TPU v7x, 32 devices: a whole 2x2x4 slice. The times are simulated.
32 devices in a mesh: tm: 4 (over y, x), lib: 8 (over z, core).
Axes of the slice: x: 2, y: 2, z: 4, core: 2. Of those that a mesh axis runs over, the one named last changes fastest.
Arguments:
- record: bfloat16 [24, 2048], P(None, 'tm'), may hold values from -6 to 6
- templates: bfloat16 [8, 4, 4, 24, 64, 256], P('lib', 'tm'), may hold values from -6 to 6
- owner: int32 [8, 2], P('lib'), may hold values from 0 to 3
- slot: int32 [8, 2], P('lib'), may hold values from 0 to 3
- mask: int32 [24], replicated, may hold values 0 or 1
Outputs:
- stacks: bfloat16 [8, 2, 64, 2048], P('lib', None, None, 'tm')
- best: float32 [2048], P('tm')
Inputs may be any that keep to these rules, and one draw needn't show every extreme that they name: owner names a tm index. slot names a held block.
All inputs are finite; a program needn't handle non-finite values.
Results may differ from a plain program's by a relative error of at most 0.005.
Values may be sent and summed in bfloat16 or wider, within the bound.
No kernel may reach another device: no remote copies, remote signals or barrier semaphores. Data moves between devices by JAX's collectives and lax.ppermute only.
A program may use at most 64 MiB of HBM per device.

v0:
```python
import jax
import jax.numpy as jnp
from jax import lax
from jax.sharding import PartitionSpec as P


def shifted(x, axis, by):
    count = lax.axis_size(axis)
    pairs = [(i, i + by) for i in range(count) if 0 <= i + by < count]
    return lax.ppermute(x, axis, pairs)


def spread(value, axis, source):
    kept = jnp.where(lax.axis_index(axis) == source, value, 0).astype(value.dtype)
    return lax.psum(kept, axis)


def unfold(segment, taps, span_len):
    return jnp.stack([segment[:, k : k + span_len] for k in range(taps)], axis=1)


def on_device(record, templates, owner, slot, mask):
    channels, samples = record.shape
    tap_count = templates.shape[-1]
    block_size = templates.shape[-2]
    rounds = owner.shape[1]
    incoming = shifted(record[:, :tap_count], "tm", -1)
    extended = jnp.concatenate([record, incoming], axis=1)
    mask_f = mask.astype(jnp.float32)
    count = jnp.maximum(jnp.sum(mask_f), 1.0)
    gain = jnp.sqrt(jnp.float32(tap_count)) / jnp.sqrt(count)
    own_blocks = templates[0, 0]
    squares = extended.astype(jnp.float32) ** 2
    running = jnp.concatenate(
        [jnp.zeros((channels, 1), jnp.float32), jnp.cumsum(squares, axis=1)], axis=1
    )
    energy_all = running[:, tap_count : tap_count + samples] - running[:, :samples]
    weight_all = mask_f[:, None] / jnp.sqrt(jnp.maximum(energy_all, jnp.float32(tap_count / 4)))

    def select_block(turn):
        return lax.dynamic_index_in_dim(own_blocks, slot[0, turn], 0, keepdims=False)

    delivered = [spread(select_block(turn), "tm", owner[0, turn]) for turn in range(rounds)]
    kernels = []
    for turn in range(rounds):
        chosen = delivered[turn].astype(jnp.float32)
        norms = jnp.sqrt(jnp.sum(chosen * chosen, axis=-1, keepdims=True) + 1e-06)
        kernels.append((chosen / norms).astype(jnp.bfloat16))
    joined = jnp.concatenate(kernels, axis=1)
    span_len = 512
    window = unfold(extended, tap_count, span_len)
    corr = jnp.einsum("cmk,ckt->cmt", joined, window, preferred_element_type=jnp.float32)
    stack_f = jnp.einsum("cmt,ct->mt", corr, weight_all) * gain
    pieces = [stack_f]
    whole = jnp.concatenate(pieces, axis=1).reshape(rounds, block_size, samples)
    stacks = whole.astype(jnp.bfloat16)[None]
    local_best = jnp.max(whole.reshape(rounds * block_size, samples), axis=0)
    best = lax.pmax(local_best, "lib")
    return (stacks, best)


def solution(mesh):
    placed = (
        P(None, "tm"),
        P("lib", "tm", None, None, None, None),
        P("lib", None),
        P("lib", None),
        P(),
    )
    return jax.shard_map(
        on_device,
        mesh=mesh,
        in_specs=placed,
        out_specs=(P("lib", None, None, "tm"), P("tm")),
        check_vma=False,
    )
```

profile of v0, /device:TPU:0, one launch (start us, length us, event | category | flops | bytes accessed | tf_op | source)
XLA Modules:
  0.0 238.2 jit_solution(2508875272615897613)
XLA Ops:
  7.2 0.7 slice.792
  7.9 1.3 collective-permute-start
  9.2 1.3 fusion.18
  13.1 1.3 fusion.17
  17.0 2.7 %select_bitcast_fusion.1 = (bf16[24,64,256]{2,1,0:T(8,128)(2,1)}, bf16[24,64,256]{2,1,0:T(8,128)(2,1)}) fusion(bf16[1,1,4,24,64,256]{5,4,3,2,1,0:T(8,128)(2,1)} %param.6, s32[]{:T(128)S(6)} %select_n.28, pred[]{:T(512)S(6)} %eq.6, s32[]{:T(128)S(6)} %select_n.32, pred[]{:T(512)S(6)} %eq.7), kind=kLoop, calls=%fused_computation.15 | loop fusion | flops 786432 | bytes 3145738 | tf_op jit(solution)/shard_map/jit(_where)/select_n | solution.py:14
  19.7 0.7 constant_dynamic-update-slice_fusion.1
  20.5 1.3 constant_dynamic-update-slice_fusion.257
  21.8 1.3 convert_reduce_fusion
  24.5 0.7 constant_dynamic-update-slice_fusion.256
  30.6 0.7 constant_dynamic-update-slice_fusion.247
  32.7 0.7 constant_dynamic-update-slice_fusion.244
  35.4 0.7 constant_dynamic-update-slice_fusion.240
  36.1 0.7 constant_dynamic-update-slice_fusion.239
  38.8 0.7 constant_dynamic-update-slice_fusion.235
  40.9 0.7 constant_dynamic-update-slice_fusion.232
  47.0 0.7 constant_dynamic-update-slice_fusion.223
  49.0 0.7 constant_dynamic-update-slice_fusion.220
  49.7 0.7 constant_dynamic-update-slice_fusion.219
  51.8 0.7 constant_dynamic-update-slice_fusion.216
  54.5 0.7 constant_dynamic-update-slice_fusion.212
  57.9 0.7 constant_dynamic-update-slice_fusion.207
  65.4 0.7 constant_dynamic-update-slice_fusion.196
  66.1 0.7 constant_dynamic-update-slice_fusion.195
  71.5 0.7 constant_dynamic-update-slice_fusion.187
  73.6 0.7 constant_dynamic-update-slice_fusion.184
  74.3 0.7 constant_dynamic-update-slice_fusion.183
  77.0 0.7 constant_dynamic-update-slice_fusion.179
  79.1 0.7 constant_dynamic-update-slice_fusion.176
  79.8 0.7 constant_dynamic-update-slice_fusion.175
  82.5 0.7 constant_dynamic-update-slice_fusion.171
  92.7 0.7 constant_dynamic-update-slice_fusion.156
  98.8 0.7 constant_dynamic-update-slice_fusion.147
  101.6 0.7 constant_dynamic-update-slice_fusion.143
  102.3 0.7 constant_dynamic-update-slice_fusion.142
  112.4 0.7 constant_dynamic-update-slice_fusion.127
  115.1 0.7 constant_dynamic-update-slice_fusion.123
  123.3 0.7 constant_dynamic-update-slice_fusion.111
  128.8 0.7 constant_dynamic-update-slice_fusion.103
  136.9 0.7 constant_dynamic-update-slice_fusion.91
  141.0 0.7 constant_dynamic-update-slice_fusion.85
  153.3 0.7 constant_dynamic-update-slice_fusion.67
  155.4 0.7 constant_dynamic-update-slice_fusion.64
  161.5 0.7 constant_dynamic-update-slice_fusion.55
  163.6 0.7 constant_dynamic-update-slice_fusion.52
  167.0 0.7 constant_dynamic-update-slice_fusion.47
  169.7 0.7 constant_dynamic-update-slice_fusion.43
  175.2 0.7 constant_dynamic-update-slice_fusion.35
  177.9 0.7 constant_dynamic-update-slice_fusion.31
  179.9 0.7 constant_dynamic-update-slice_fusion.28
  180.6 0.7 constant_dynamic-update-slice_fusion.27
  182.7 0.7 constant_dynamic-update-slice_fusion.24
  186.1 0.7 constant_dynamic-update-slice_fusion.19
  188.2 0.7 constant_dynamic-update-slice_fusion.16
  190.9 0.7 constant_dynamic-update-slice_fusion.12
  191.6 0.7 constant_dynamic-update-slice_fusion.11
  194.3 0.7 constant_dynamic-update-slice_fusion.7
  195.0 1.7 reduce-window.6
  198.3 0.7 constant_dynamic-update-slice_fusion.4
  199.0 0.7 constant_dynamic-update-slice_fusion.3
  200.6 1.9 fusion.4
  202.4 1.4 fusion.5
  203.9 1.4 fusion.7
  205.3 6.7 %multiply_reduce_fusion = f32[512,128]{0,1:T(8,128)S(1)} fusion(f32[512,24]{0,1:T(8,128)S(1)} %fusion.15, bf16[24,256,512]{2,0,1:T(8,128)(2,1)} %constant_dynamic-update-slice_fusion.2, bf16[24,64,256]{2,1,0:T(8,128)(2,1)S(1)} %fusion.7, bf16[24,64,256]{2,1,0:T(8,128)(2,1)S(1)} %fusion.5), kind=kOutput, calls=%fused_computation | convolution fusion | flops 811532288 | bytes 8175616 | tf_op jit(solution)/shard_map/cmk,ckt->cmt/dot_general | solution.py:52
  212.7 18.7 %pmax.7 = f32[512]{0:T(512)} all-reduce(f32[512]{0:T(512)S(1)} %get-tuple-element.6), channel_id=1, replica_groups=mesh['tm'=4,'lib'=8] {'lib'}, use_global_device_ids=true, to_apply=%region_8.9 | all-reduce | flops 512 | bytes 4096 | tf_op jit(solution)/shard_map/pmax | solution.py:58
  (219 shorter events, 141.1 us)
Async XLA Ops:
  7.2 193.4 %all-reduce.4.cloned.1.call-start = ((), (), s32[]{:S(2)}) async-start(), calls=%async_computation | async-start | bytes 3145728 | tf_op jit(solution)/shard_map/psum | solution.py:15
  7.9 16.5 %collective-permute-start = (bf16[24,256]{1,0:T(8,128)(2,1)S(1)}, bf16[24,256]{1,0:T(8,128)(2,1)S(1)}, u32[]{:S(2)}, u32[]{:S(2)}) collective-permute-start(bf16[24,256]{1,0:T(8,128)(2,1)S(1)} %slice.792), channel_id=1, source_target_pairs={{8,0},{16,8},{24,16},{9,1},{17,9},{25,17},{10,2},{18,10},{26,18},{... | collective-permute-start | bytes 36872 | tf_op jit(solution)/shard_map/ppermute | solution.py:10
Sparse Core Ops, SparseCore 0:
  19.9 64.9 all-reduce.3
where the time goes:
time: 239 us; the launch traced here: 238 us
  local copies, waits for them, and re-layouts  179 us (75%)
  between operations  20.1 us (8%)
  blocking collectives  18.7 us (8%)
  other arithmetic  11.9 us (5%)
  matrix products  6.7 us (3%)
    unnamed x256, local copies, waits for them, and re-layouts  175 us
    pmax x1, blocking collectives, on_device(): best = lax.pmax(local_best, 'lib')  18.7 us
    dot_general x1, matrix products, on_device(): jnp.einsum('cmk,ckt->cmt', joined, window, preferred_element_type=jnp.flo...  6.7 us
  transfers between devices with their start and end apart: 2, of which 0 were waited for; matrix products, arithmetic and copies ran while one was open for 78% of the time, Pallas kernels for 0%

commit v1 on v0

v1 whole, which is shorter than its diff:
```python
import functools

import jax
import jax.numpy as jnp
from jax import lax
from jax.experimental import pallas as pl
from jax.experimental.pallas import tpu as pltpu
from jax.sharding import PartitionSpec as P

F32 = jnp.float32
BF16 = jnp.bfloat16
VMEM = pltpu.VMEM
SMEM = pltpu.SMEM


def swap(x, axis, flip):
    count = lax.axis_size(axis)
    return lax.ppermute(x, axis, [(i, i ^ flip) for i in range(count)])


def owns_any(owner_ref, me, rounds):
    mine = owner_ref[0, 0] == me
    for turn in range(1, rounds):
        mine = jnp.logical_or(mine, owner_ref[0, turn] == me)
    return mine


def prepare(me_ref, owner_ref, slot_ref, templates_ref, units_ref, held, sems):
    rounds, channels, block, taps = held.shape

    @pl.when(owns_any(owner_ref, me_ref[0], rounds))
    def _():
        copies = [
            pltpu.make_async_copy(templates_ref.at[slot_ref[0, r]], held.at[r], sems.at[r])
            for r in range(rounds)
        ]
        for copy in copies:
            copy.start()
        row = lax.broadcasted_iota(jnp.int32, (taps, taps), 0)
        col = lax.broadcasted_iota(jnp.int32, (taps, taps), 1)
        mirror = jnp.where(row + col == taps - 1, 1.0, 0.0).astype(BF16)
        for r in range(rounds):
            copies[r].wait()
            for c in range(channels):
                chosen = held[r, c]
                wide = chosen.astype(F32)
                norm = jnp.sum(wide * wide, axis=-1, keepdims=True) + 1e-06
                turned = jnp.dot(chosen, mirror, preferred_element_type=F32)
                units_ref[c, r * block : (r + 1) * block, :] = (turned * lax.rsqrt(norm)).astype(BF16)


def correlate(me_ref, owner_ref, mask_ref, *refs):
    *part_refs, units_ref, out_ref, spans = refs
    shards = len(part_refs)
    channels, samples = part_refs[0].shape
    rows, taps = units_ref.shape[1:]
    rounds = owner_ref.shape[1]
    me = me_ref[0]

    @pl.when(owns_any(owner_ref, me, rounds))
    def _():
        for d in range(shards):
            spans[me ^ d] = part_refs[d][...]
        spans[shards] = jnp.zeros((channels, samples), BF16)
        count = mask_ref[0]
        for c in range(1, channels):
            count = count + mask_ref[c]
        alive = jnp.maximum(jnp.full((8, 128), count, jnp.int32).astype(F32), 1.0)
        gain = (jnp.sqrt(F32(taps)) * lax.rsqrt(alive))[:1, :1]

        def shard(d, carry):
            j = me ^ d
            span = jnp.concatenate([spans[j], spans[j + 1][:, :taps]], axis=1)
            width = samples + taps
            wide = span.astype(F32)
            energy = wide * wide
            reach = 1
            while reach < taps:
                energy = energy + pltpu.roll(energy, width - reach, 1)
                reach *= 2
            weight = gain * lax.rsqrt(jnp.maximum(energy[:, :samples], F32(taps / 4)))
            total = jnp.zeros((rows, samples), F32)
            for c in range(channels):
                line = jnp.broadcast_to(span[c : c + 1, :], (taps // 2, width))
                slid = pltpu.roll(line, width - (taps // 2 - 1), 1, stride=1, stride_axis=0)
                window = jnp.concatenate(
                    [slid[:, taps // 2 : taps // 2 + samples], slid[:, :samples]], axis=0
                )
                corr = jnp.dot(units_ref[c], window, preferred_element_type=F32)
                total = total + corr * (weight[c : c + 1, :] * mask_ref[c].astype(F32))
            out_ref[d] = total.astype(BF16)
            return carry

        lax.fori_loop(0, shards, shard, 0)


def combine(me_ref, owner_ref, *refs):
    *held_refs, out_ref, best_ref = refs
    rounds, block, samples = out_ref.shape
    for r in range(rounds):
        source = owner_ref[0, r] ^ me_ref[0]
        for d, ref in enumerate(held_refs):

            @pl.when(source == d)
            def _():
                out_ref[r] = ref[r * block : (r + 1) * block, :]

    best_ref[...] = jnp.max(
        out_ref[...].astype(F32).reshape(rounds * block, samples), axis=0, keepdims=True
    )


def spec(space):
    return pl.BlockSpec(memory_space=space)


def on_device(record, templates, owner, slot, mask):
    channels, samples = record.shape
    slots, _, block, taps = templates.shape[2:]
    rounds = owner.shape[1]
    shards = lax.axis_size("tm")
    rows = rounds * block
    me = lax.axis_index("tm").astype(jnp.int32).reshape(1)

    parts = [record] + [swap(record, "tm", d) for d in range(1, shards)]

    units = pl.pallas_call(
        prepare,
        out_shape=jax.ShapeDtypeStruct((channels, rows, taps), BF16),
        in_specs=[spec(SMEM)] * 3 + [spec(pl.ANY)],
        out_specs=spec(VMEM),
        scratch_shapes=[
            VMEM((rounds, channels, block, taps), BF16),
            pltpu.SemaphoreType.DMA((rounds,)),
        ],
        compiler_params=pltpu.CompilerParams(vmem_limit_bytes=16 << 20),
        cost_estimate=pl.CostEstimate(flops=4 * 10**8, bytes_accessed=3 << 20, transcendentals=0),
        name="prepare",
    )(me, owner, slot, templates[0, 0])

    stacked = pl.pallas_call(
        correlate,
        out_shape=jax.ShapeDtypeStruct((shards, rows, samples), BF16),
        in_specs=[spec(SMEM)] * 3 + [spec(VMEM)] * (shards + 1),
        out_specs=spec(VMEM),
        scratch_shapes=[VMEM((shards + 1, channels, samples), BF16)],
        compiler_params=pltpu.CompilerParams(vmem_limit_bytes=24 << 20),
        name="correlate",
    )(me, owner, mask, *parts, units)

    held = [stacked[0]] + [swap(stacked[d], "tm", d) for d in range(1, shards)]

    stacks, best = pl.pallas_call(
        combine,
        out_shape=(
            jax.ShapeDtypeStruct((rounds, block, samples), BF16),
            jax.ShapeDtypeStruct((1, samples), F32),
        ),
        in_specs=[spec(SMEM)] * 2 + [spec(VMEM)] * shards,
        out_specs=(spec(VMEM), spec(VMEM)),
        compiler_params=pltpu.CompilerParams(vmem_limit_bytes=16 << 20),
        name="combine",
    )(me, owner, *held)

    rows_count = lax.axis_size("lib")
    step = 1
    while step < rows_count:
        flips = [step] if step == 1 or 2 * step >= rows_count else [step, 2 * step, 3 * step]
        others = [swap(best, "lib", flip) for flip in flips]
        best = functools.reduce(jnp.maximum, others, best)
        step *= 1 + len(flips)
    return stacks[None], best[0]


def solution(mesh):
    placed = (
        P(None, "tm"),
        P("lib", "tm", None, None, None, None),
        P("lib", None),
        P("lib", None),
        P(),
    )
    return jax.shard_map(
        on_device,
        mesh=mesh,
        in_specs=placed,
        out_specs=(P("lib", None, None, "tm"), P("tm")),
        check_vma=False,
    )
```

time: 239 us -> 39.4 us (0.16)
  local copies, waits for them, and re-layouts: 179 us -> 3.25 us
  between operations: 20.1 us -> 0.73 us
  blocking collectives: 18.7 us -> 0 us
  Pallas kernels: 0 us -> 12.3 us
  other arithmetic: 11.9 us -> 0.59 us
  starting transfers between devices: 1.32 us -> 12.5 us
  waiting for transfers between devices: 0.04 us -> 9.64 us
  matrix products: 6.7 us -> 0 us
    unnamed x256 -> x12, local copies, waits for them, and re-layouts: 175 us -> 3.21 us
    pmax x1 -> x0, blocking collectives: 18.7 us -> none  [on_device(): best = lax.pmax(local_best, 'lib')]
    pallas_call x0 -> x3, Pallas kernels: none -> 12.3 us  [the longest x1 9.06 us: on_device(): pl.pallas_call(correlate, out_shape=jax.ShapeDtypeStruct((shards, rows, s...]
    ppermute x1 -> x10, starting transfers between devices: 1.28 us -> 12.5 us  [swap(): return lax.ppermute(x, axis, [(i, i ^ flip) for i in range(count)])]
    ppermute x1 -> x10, waiting for transfers between devices: 0.01 us -> 9.64 us  [swap(): return lax.ppermute(x, axis, [(i, i ^ flip) for i in range(count)])]
    dot_general x1 -> x0, matrix products: 6.7 us -> none  [on_device(): jnp.einsum('cmk,ckt->cmt', joined, window, preferred_element_type=jnp.flo...]
    slice x4 -> x0, local copies, waits for them, and re-layouts: 3.52 us -> none  [the longest x1 1.33 us: on_device(): owner[0, turn]]
    convert_element_type x3 -> x0, other arithmetic: 3.47 us -> none  [the longest x2 2.81 us: on_device(): kernels.append((chosen / norms).astype(jnp.bfloat16))]
  transfers between devices with their start and end apart: 2 -> 10, of which waited for: 0 -> 5; matrix products, arithmetic and copies ran while one was open for 78% -> 0% of each run, Pallas kernels for 0% -> 5%
where the time goes in v1:
time: 39.4 us; the launch traced here: 39.1 us
  starting transfers between devices  12.5 us (32%)
  Pallas kernels  12.3 us (31%)
  waiting for transfers between devices  9.64 us (24%)
  local copies, waits for them, and re-layouts  3.25 us (8%)
  between operations  0.73 us (2%)
  other arithmetic  0.59 us (1%)
    ppermute x10, starting transfers between devices, swap(): return lax.ppermute(x, axis, [(i, i ^ flip) for i in range(count)])  12.5 us
    ppermute x10, waiting for transfers between devices, swap(): return lax.ppermute(x, axis, [(i, i ^ flip) for i in range(count)])  9.64 us
    pallas_call x1, Pallas kernels, on_device(): pl.pallas_call(correlate, out_shape=jax.ShapeDtypeStruct((shards, rows, s...  9.06 us
    unnamed x12, local copies, waits for them, and re-layouts  3.21 us
    pallas_call x1, Pallas kernels, on_device(): pl.pallas_call(prepare, out_shape=jax.ShapeDtypeStruct((channels, rows, t...  2.02 us
    pallas_call x1, Pallas kernels, on_device(): pl.pallas_call(combine, out_shape=(jax.ShapeDtypeStruct((rounds, block, s...  1.24 us
  transfers between devices with their start and end apart: 10, of which 5 were waited for; matrix products, arithmetic and copies ran while one was open for 0% of the time, Pallas kernels for 5%

profile of v1, /device:TPU:0, one launch (start us, length us, event | category | flops | bytes accessed | tf_op | source)
XLA Modules:
  0.0 39.1 jit_solution(16662962853191283819)
XLA Ops:
  0.6 0.0 copy-start.3
  0.6 0.0 copy-start.4
  0.7 3.0 %collective-permute-start.1 = (bf16[24,512]{1,0:T(8,128)(2,1)}, bf16[24,512]{1,0:T(8,128)(2,1)S(1)}, u32[]{:S(2)}, u32[]{:S(2)}) collective-permute-start(bf16[24,512]{1,0:T(8,128)(2,1)} %refs_0_.1), channel_id=1, source_target_pairs={{0,16},{8,24},{16,0},{24,8},{1,17},{9,25},{17,1},{25,9},{2,18},{10... | collective-permute-start | bytes 73736 | tf_op jit(solution)/shard_map/ppermute | solution.py:18
  3.7 1.5 %collective-permute-start = (bf16[24,512]{1,0:T(8,128)(2,1)}, bf16[24,512]{1,0:T(8,128)(2,1)S(1)}, u32[]{:S(2)}, u32[]{:S(2)}) collective-permute-start(bf16[24,512]{1,0:T(8,128)(2,1)} %refs_0_.1), channel_id=1, source_target_pairs={{0,8},{8,0},{16,24},{24,16},{1,9},{9,1},{17,25},{25,17},{2,10},{10... | collective-permute-start | bytes 73736 | tf_op jit(solution)/shard_map/ppermute | solution.py:18
  5.2 0.0 collective-permute-start.2
  5.2 0.0 copy-start
  5.2 1.9 %copy-done = bf16[1,1,4,24,64,256]{5,4,3,2,1,0:T(8,128)(2,1)S(1)} copy-done((bf16[1,1,4,24,64,256]{5,4,3,2,1,0:T(8,128)(2,1)S(1)}, bf16[1,1,4,24,64,256]{5,4,3,2,1,0:T(8,128)(2,1)}, u32[]{:S(2)}) %copy-start) | copy-done | bytes 3145752
  7.1 0.0 copy-start.2
  7.1 0.7 %copy-done.2 = s32[1,2]{1,0:T(1,128)S(1)} copy-done((s32[1,2]{1,0:T(1,128)S(1)}, s32[1,2]{1,0:T(1,128)}, u32[]{:S(2)}) %copy-start.2) | copy-done | bytes 32
  7.8 0.0 copy-start.5
  7.8 0.7 %copy-done.5 = s32[1,2]{1,0:T(1,128)S(1)} copy-done((s32[1,2]{1,0:T(1,128)S(1)}, s32[1,2]{1,0:T(1,128)}, u32[]{:S(2)}) %copy-start.5) | copy-done | bytes 32
  8.4 0.0 copy-start.1
  8.4 2.0 %prepare.1.refs_4_ = bf16[24,128,256]{2,1,0:T(8,128)(2,1)S(1)} custom-call(s32[1]{0:T(128)} %bitcast.me_ref, s32[1,2]{1,0:T(1,128)S(1)} %copy-done.2, s32[1,2]{1,0:T(1,128)S(1)} %copy-done.5, bf16[4,24,64,256]{3,2,1,0:T(8,128)(2,1)S(1)} %bitcast.12), custom_call_target="tpu_custom_call" | custom-call | flops 400000000 | bytes 3145728 | tf_op jit(solution)/shard_map/prepare/pallas_call | solution.py:127
  10.5 0.0 collective-permute-done.1.refs_2_
  10.5 0.0 collective-permute-done.refs_1_
  10.5 0.0 collective-permute-done.2.refs_3_
  10.5 0.0 copy-done.3
  10.5 0.0 copy-done.4
  10.5 0.0 copy-done.1
  10.5 9.1 %correlate.1 = bf16[4,128,512]{2,1,0:T(8,128)(2,1)S(1)} custom-call(s32[1]{0:T(128)} %bitcast.me_ref, s32[1,2]{1,0:T(1,128)S(1)} %copy-done.3, s32[24]{0:T(128)S(1)} %copy-done.4, bf16[24,512]{1,0:T(8,128)(2,1)S(1)} %copy-done.1, bf16[24,512]{1,0:T(8,128)(2,1)S(1)} %collective-permute-done.refs_1_, bf16[24,512]{1,0:T(8,128)(2,1)S(1)} %collective-permute-done.1.refs_2_, ...), custom_call_target="tpu_custom_call" | custom-call | tf_op jit(solution)/shard_map/correlate/pallas_call | solution.py:141
  19.6 2.9 %collective-permute-start.5 = (bf16[128,512]{1,0:T(8,128)(2,1)S(1)}, bf16[128,512]{1,0:T(8,128)(2,1)S(1)}, u32[]{:S(2)}, u32[]{:S(2)}) collective-permute-start(bf16[128,512]{1,0:T(8,128)(2,1)S(1)} %get-tuple-element.6), channel_id=1, source_target_pairs={{0,24},{8,16},{16,8},{24,0},{1,25},{9,17},{17,9},{25,1},{2,26},{10... | collective-permute-start | bytes 393224 | tf_op jit(solution)/shard_map/ppermute | solution.py:18
  22.6 0.0 collective-permute-start.4
  22.6 0.6 %collective-permute-start.3 = (bf16[128,512]{1,0:T(8,128)(2,1)S(1)}, bf16[128,512]{1,0:T(8,128)(2,1)S(1)}, u32[]{:S(2)}, u32[]{:S(2)}) collective-permute-start(bf16[128,512]{1,0:T(8,128)(2,1)S(1)} %get-tuple-element.8), channel_id=1, source_target_pairs={{0,8},{8,0},{16,24},{24,16},{1,9},{9,1},{17,25},{25,17},{2,10},{10... | collective-permute-start | bytes 393224 | tf_op jit(solution)/shard_map/ppermute | solution.py:18
  23.2 3.5 %collective-permute-done.5.refs_3_ = bf16[128,512]{1,0:T(8,128)(2,1)S(1)} collective-permute-done((bf16[128,512]{1,0:T(8,128)(2,1)S(1)}, bf16[128,512]{1,0:T(8,128)(2,1)S(1)}, u32[]{:S(2)}, u32[]{:S(2)}) %collective-permute-start.5) | collective-permute-done | bytes 131104 | tf_op jit(solution)/shard_map/ppermute | solution.py:18
  26.7 1.4 %collective-permute-done.4.refs_2_ = bf16[128,512]{1,0:T(8,128)(2,1)S(1)} collective-permute-done((bf16[128,512]{1,0:T(8,128)(2,1)S(1)}, bf16[128,512]{1,0:T(8,128)(2,1)S(1)}, u32[]{:S(2)}, u32[]{:S(2)}) %collective-permute-start.4) | collective-permute-done | bytes 131104 | tf_op jit(solution)/shard_map/ppermute | solution.py:18
  28.1 0.0 collective-permute-done.3.refs_1_
  28.1 1.2 %combine.1 = (bf16[2,64,512]{2,1,0:T(8,128)(2,1)}, f32[1,512]{1,0:T(1,128)S(1)}) custom-call(s32[1]{0:T(128)} %bitcast.me_ref, s32[1,2]{1,0:T(1,128)S(1)} %copy-done.3, bf16[128,512]{1,0:T(8,128)(2,1)S(1)} %get-tuple-element.9.refs_0_, bf16[128,512]{1,0:T(8,128)(2,1)S(1)} %collective-permute-done.3.refs_1_, ...), custom_call_target="tpu_custom_call" | custom-call | tf_op jit(solution)/shard_map/combine/pallas_call | solution.py:153
  29.3 0.0 collective-permute-start.6
  29.3 1.2 %collective-permute-done.6 = f32[1,512]{1,0:T(1,128)S(1)} collective-permute-done((f32[1,512]{1,0:T(1,128)S(1)}, f32[1,512]{1,0:T(1,128)S(1)}, u32[]{:S(2)}, u32[]{:S(2)}) %collective-permute-start.6) | collective-permute-done | bytes 2080 | tf_op jit(solution)/shard_map/ppermute | solution.py:18
  30.5 3.5 %collective-permute-start.9 = (f32[1,512]{1,0:T(1,128)S(1)}, f32[1,512]{1,0:T(1,128)S(1)}, u32[]{:S(2)}, u32[]{:S(2)}) collective-permute-start(f32[1,512]{1,0:T(1,128)S(1)} %max.12), channel_id=1, source_target_pairs={{0,6},{1,7},{2,4},{3,5},{4,2},{5,3},{6,0},{7,1},{8,14},{9,15},{10,... | collective-permute-start | bytes 6152 | tf_op jit(solution)/shard_map/ppermute | solution.py:18
  34.0 0.0 collective-permute-start.8
  34.0 0.9 %collective-permute-start.7 = (f32[1,512]{1,0:T(1,128)S(1)}, f32[1,512]{1,0:T(1,128)S(1)}, u32[]{:S(2)}, u32[]{:S(2)}) collective-permute-start(f32[1,512]{1,0:T(1,128)S(1)} %max.12), channel_id=1, source_target_pairs={{0,2},{1,3},{2,0},{3,1},{4,6},{5,7},{6,4},{7,5},{8,10},{9,11},{10,... | collective-permute-start | bytes 6152 | tf_op jit(solution)/shard_map/ppermute | solution.py:18
  34.9 1.0 %collective-permute-done.9 = f32[1,512]{1,0:T(1,128)S(1)} collective-permute-done((f32[1,512]{1,0:T(1,128)S(1)}, f32[1,512]{1,0:T(1,128)S(1)}, u32[]{:S(2)}, u32[]{:S(2)}) %collective-permute-start.9) | collective-permute-done | bytes 2080 | tf_op jit(solution)/shard_map/ppermute | solution.py:18
  35.9 2.6 %collective-permute-done.8 = f32[1,512]{1,0:T(1,128)S(1)} collective-permute-done((f32[1,512]{1,0:T(1,128)S(1)}, f32[1,512]{1,0:T(1,128)S(1)}, u32[]{:S(2)}, u32[]{:S(2)}) %collective-permute-start.8) | collective-permute-done | bytes 2080 | tf_op jit(solution)/shard_map/ppermute | solution.py:18
  38.5 0.0 collective-permute-done.7
  38.5 0.6 %maximum_maximum_fusion = f32[1,512]{1,0:T(1,128)} fusion(f32[1,512]{1,0:T(1,128)S(1)} %collective-permute-done.9, f32[1,512]{1,0:T(1,128)S(1)} %collective-permute-done.8, f32[1,512]{1,0:T(1,128)S(1)} %max.12, f32[1,512]{1,0:T(1,128)S(1)} %collective-permute-done.7), kind=kLoop, calls=%fused_computation.4 | loop fusion | flops 1536 | bytes 10240 | tf_op jit(solution)/shard_map/max | solution.py:170
  (2 shorter events, 0.0 us)
Async XLA Ops:
  0.6 9.9 %copy-start.3 = (s32[1,2]{1,0:T(1,128)S(1)}, s32[1,2]{1,0:T(1,128)}, u32[]{:S(2)}) copy-start(s32[1,2]{1,0:T(1,128)} %owner_ref.5) | copy-start | bytes 28
  0.6 9.9 %copy-start.4 = (s32[24]{0:T(128)S(1)}, s32[24]{0:T(128)}, u32[]{:S(2)}) copy-start(s32[24]{0:T(128)} %mask_ref.1) | copy-start | bytes 292
  0.7 9.8 %collective-permute-start.1 = (bf16[24,512]{1,0:T(8,128)(2,1)}, bf16[24,512]{1,0:T(8,128)(2,1)S(1)}, u32[]{:S(2)}, u32[]{:S(2)}) collective-permute-start(bf16[24,512]{1,0:T(8,128)(2,1)} %refs_0_.1), channel_id=1, source_target_pairs={{0,16},{8,24},{16,0},{24,8},{1,17},{9,25},{17,1},{25,9},{2,18},{10... | collective-permute-start | bytes 73736 | tf_op jit(solution)/shard_map/ppermute | solution.py:18
  3.7 6.8 %collective-permute-start = (bf16[24,512]{1,0:T(8,128)(2,1)}, bf16[24,512]{1,0:T(8,128)(2,1)S(1)}, u32[]{:S(2)}, u32[]{:S(2)}) collective-permute-start(bf16[24,512]{1,0:T(8,128)(2,1)} %refs_0_.1), channel_id=1, source_target_pairs={{0,8},{8,0},{16,24},{24,16},{1,9},{9,1},{17,25},{25,17},{2,10},{10... | collective-permute-start | bytes 73736 | tf_op jit(solution)/shard_map/ppermute | solution.py:18
  5.2 5.3 %collective-permute-start.2 = (bf16[24,512]{1,0:T(8,128)(2,1)}, bf16[24,512]{1,0:T(8,128)(2,1)S(1)}, u32[]{:S(2)}, u32[]{:S(2)}) collective-permute-start(bf16[24,512]{1,0:T(8,128)(2,1)} %refs_0_.1), channel_id=1, source_target_pairs={{0,24},{8,16},{16,8},{24,0},{1,25},{9,17},{17,9},{25,1},{2,26},{10... | collective-permute-start | bytes 73736 | tf_op jit(solution)/shard_map/ppermute | solution.py:18
  5.2 1.9 %copy-start = (bf16[1,1,4,24,64,256]{5,4,3,2,1,0:T(8,128)(2,1)S(1)}, bf16[1,1,4,24,64,256]{5,4,3,2,1,0:T(8,128)(2,1)}, u32[]{:S(2)}) copy-start(bf16[1,1,4,24,64,256]{5,4,3,2,1,0:T(8,128)(2,1)} %param.6) | copy-start | bytes 9437188
  7.1 0.7 %copy-start.2 = (s32[1,2]{1,0:T(1,128)S(1)}, s32[1,2]{1,0:T(1,128)}, u32[]{:S(2)}) copy-start(s32[1,2]{1,0:T(1,128)} %owner_ref.5) | copy-start | bytes 28
  7.8 0.7 %copy-start.5 = (s32[1,2]{1,0:T(1,128)S(1)}, s32[1,2]{1,0:T(1,128)}, u32[]{:S(2)}) copy-start(s32[1,2]{1,0:T(1,128)} %slot_ref.1) | copy-start | bytes 28
  8.4 2.1 %copy-start.1 = (bf16[24,512]{1,0:T(8,128)(2,1)S(1)}, bf16[24,512]{1,0:T(8,128)(2,1)}, u32[]{:S(2)}) copy-start(bf16[24,512]{1,0:T(8,128)(2,1)} %refs_0_.1) | copy-start | bytes 73732
  19.6 7.1 %collective-permute-start.5 = (bf16[128,512]{1,0:T(8,128)(2,1)S(1)}, bf16[128,512]{1,0:T(8,128)(2,1)S(1)}, u32[]{:S(2)}, u32[]{:S(2)}) collective-permute-start(bf16[128,512]{1,0:T(8,128)(2,1)S(1)} %get-tuple-element.6), channel_id=1, source_target_pairs={{0,24},{8,16},{16,8},{24,0},{1,25},{9,17},{17,9},{25,1},{2,26},{10... | collective-permute-start | bytes 393224 | tf_op jit(solution)/shard_map/ppermute | solution.py:18
  22.6 5.5 %collective-permute-start.4 = (bf16[128,512]{1,0:T(8,128)(2,1)S(1)}, bf16[128,512]{1,0:T(8,128)(2,1)S(1)}, u32[]{:S(2)}, u32[]{:S(2)}) collective-permute-start(bf16[128,512]{1,0:T(8,128)(2,1)S(1)} %get-tuple-element.7), channel_id=1, source_target_pairs={{0,16},{8,24},{16,0},{24,8},{1,17},{9,25},{17,1},{25,9},{2,18},{10... | collective-permute-start | bytes 393224 | tf_op jit(solution)/shard_map/ppermute | solution.py:18
  22.6 5.5 %collective-permute-start.3 = (bf16[128,512]{1,0:T(8,128)(2,1)S(1)}, bf16[128,512]{1,0:T(8,128)(2,1)S(1)}, u32[]{:S(2)}, u32[]{:S(2)}) collective-permute-start(bf16[128,512]{1,0:T(8,128)(2,1)S(1)} %get-tuple-element.8), channel_id=1, source_target_pairs={{0,8},{8,0},{16,24},{24,16},{1,9},{9,1},{17,25},{25,17},{2,10},{10... | collective-permute-start | bytes 393224 | tf_op jit(solution)/shard_map/ppermute | solution.py:18
  29.3 1.2 %collective-permute-start.6 = (f32[1,512]{1,0:T(1,128)S(1)}, f32[1,512]{1,0:T(1,128)S(1)}, u32[]{:S(2)}, u32[]{:S(2)}) collective-permute-start(f32[1,512]{1,0:T(1,128)S(1)} %get-tuple-element.5), channel_id=1, source_target_pairs={{0,1},{1,0},{2,3},{3,2},{4,5},{5,4},{6,7},{7,6},{8,9},{9,8},{10,11... | collective-permute-start | bytes 6152 | tf_op jit(solution)/shard_map/ppermute | solution.py:18
  30.5 5.4 %collective-permute-start.9 = (f32[1,512]{1,0:T(1,128)S(1)}, f32[1,512]{1,0:T(1,128)S(1)}, u32[]{:S(2)}, u32[]{:S(2)}) collective-permute-start(f32[1,512]{1,0:T(1,128)S(1)} %max.12), channel_id=1, source_target_pairs={{0,6},{1,7},{2,4},{3,5},{4,2},{5,3},{6,0},{7,1},{8,14},{9,15},{10,... | collective-permute-start | bytes 6152 | tf_op jit(solution)/shard_map/ppermute | solution.py:18
  34.0 4.5 %collective-permute-start.8 = (f32[1,512]{1,0:T(1,128)S(1)}, f32[1,512]{1,0:T(1,128)S(1)}, u32[]{:S(2)}, u32[]{:S(2)}) collective-permute-start(f32[1,512]{1,0:T(1,128)S(1)} %max.12), channel_id=1, source_target_pairs={{0,4},{1,5},{2,6},{3,7},{4,0},{5,1},{6,2},{7,3},{8,12},{9,13},{10,... | collective-permute-start | bytes 6152 | tf_op jit(solution)/shard_map/ppermute | solution.py:18
  34.0 4.5 %collective-permute-start.7 = (f32[1,512]{1,0:T(1,128)S(1)}, f32[1,512]{1,0:T(1,128)S(1)}, u32[]{:S(2)}, u32[]{:S(2)}) collective-permute-start(f32[1,512]{1,0:T(1,128)S(1)} %max.12), channel_id=1, source_target_pairs={{0,2},{1,3},{2,0},{3,1},{4,6},{5,7},{6,4},{7,5},{8,10},{9,11},{10,... | collective-permute-start | bytes 6152 | tf_op jit(solution)/shard_map/ppermute | solution.py:18

commit v2 on v1

v2 whole, which is shorter than its diff:
```python
import functools

import jax
import jax.numpy as jnp
from jax import lax
from jax.experimental import pallas as pl
from jax.experimental.pallas import tpu as pltpu
from jax.sharding import PartitionSpec as P

F32 = jnp.float32
BF16 = jnp.bfloat16
VMEM = pltpu.VMEM
SMEM = pltpu.SMEM
HBM = pltpu.HBM
CHUNKS = 2
TAIL = 16
PREPARE_VMEM = 51 << 20


def swap(x, axis, flip):
    count = lax.axis_size(axis)
    return lax.ppermute(x, axis, [(i, i ^ flip) for i in range(count)])


def pick(row, at):
    lane = lax.broadcasted_iota(jnp.int32, row.shape, 1)
    return jnp.sum(jnp.where(lane == at, row, 0))


def owned(owner_ref):
    return (owner_ref[...] == lax.axis_index("tm")).astype(jnp.int32)


def prepare(slot_ref, templates_ref, units_ref, held, sems):
    rounds, channels, block, taps = held.shape
    half = taps // 2
    chunks = sems.shape[1]
    step = channels // chunks

    slots = [pick(slot_ref[...], r) for r in range(rounds)]

    def fetch(r, k):
        part = pl.ds(k * step, step)
        return pltpu.make_async_copy(
            templates_ref.at[slots[r], part], held.at[r, part], sems.at[r, k]
        )

    for k in range(chunks):
        for r in range(rounds):
            fetch(r, k).start()
    row = lax.broadcasted_iota(jnp.int32, (half, half), 0)
    col = lax.broadcasted_iota(jnp.int32, (half, half), 1)
    mirror = jnp.where(row + col == half - 1, 1.0, 0.0).astype(BF16)
    for k in range(chunks):
        for r in range(rounds):
            fetch(r, k).wait()
        for c in range(k * step, (k + 1) * step):
            halves = [held[r, c, :, at : at + half] for r in range(rounds) for at in (0, half)]
            turned = jnp.dot(
                jnp.concatenate(halves, axis=0), mirror, preferred_element_type=F32
            )
            for r in range(rounds):
                wide = held[r, c].astype(F32)
                scale = lax.rsqrt(jnp.sum(wide * wide, axis=-1, keepdims=True) + 1e-06)
                for i, at in enumerate((0, half)):
                    first = (2 * r + i) * block
                    units_ref[c, r * block : (r + 1) * block, at : at + half] = (
                        turned[first : first + block] * scale
                    ).astype(BF16)


def correlate(flip, shards, ride, owner_ref, mask_ref, *refs):
    part_refs, refs = refs[:shards], refs[shards:]
    units_ref, out_ref, *refs = refs
    peak_ref = None if ride else refs.pop(0)
    spans, lines, weights = refs
    channels, samples = part_refs[0].shape
    rows, taps = units_ref.shape[1:]
    rounds = owner_ref.shape[1]
    half = taps // 2
    width = samples + taps
    lanes = 128
    me = lax.axis_index("tm")
    held = owned(owner_ref)
    mine = jnp.max(held) > 0

    def report(peak):
        if ride:
            out_ref[rows:] = jnp.broadcast_to(peak, (TAIL, samples)).astype(BF16)
        else:
            peak_ref[...] = peak

    @pl.when(jnp.logical_not(mine))
    def _():
        report(jnp.full((1, samples), -jnp.inf, F32))

    @pl.when(mine)
    def _():
        spans[shards] = jnp.zeros((channels, samples), BF16)
        for d in range(shards):
            spans[me ^ d] = part_refs[d][...]
        row = lax.broadcasted_iota(jnp.int32, (channels, channels), 0)
        col = lax.broadcasted_iota(jnp.int32, (channels, channels), 1)
        live = jnp.where(row == col, jnp.broadcast_to(mask_ref[...], row.shape), 0)
        live = jnp.sum(live, axis=1, keepdims=True).astype(F32)
        alive = jnp.maximum(jnp.sum(live, axis=0, keepdims=True), 1.0)
        gain = jnp.sqrt(F32(taps)) * lax.rsqrt(alive) * live
        lane = lax.broadcasted_iota(jnp.int32, (8, lanes), 1)
        behind = lane + lax.broadcasted_iota(jnp.int32, (8, lanes), 0)

        def build(c):
            line = lines[c]
            groups = []
            for g in range(half // 8):
                shift = half - 1 - 8 * g
                tiles = []
                for q in range(0, samples + half, lanes):
                    near, far = line[:, q : q + lanes], line[:, q + lanes : q + 2 * lanes]
                    mixed = jnp.where(behind >= shift, near, far)
                    tiles.append(pltpu.roll(mixed, lanes - shift, 1, stride=1, stride_axis=0))
                groups.append(jnp.concatenate(tiles, axis=1))
            return jnp.concatenate(groups, axis=0).astype(BF16)

        j = me ^ flip
        wide = jnp.concatenate([spans[j], spans[j + 1][:, :taps]], axis=1).astype(F32)
        energy = wide * wide
        reach = 1
        while reach < taps:
            energy = energy + pltpu.roll(energy, width - reach, 1)
            reach *= 2
        weight = gain * lax.rsqrt(jnp.maximum(energy[:, :samples], F32(taps / 4)))
        for c in range(channels):
            lines[c] = jnp.broadcast_to(wide[c : c + 1], (8, width))
            weights[c] = jnp.broadcast_to(weight[c : c + 1], (8, samples))
        stack = jnp.zeros((rows // 8, 8, samples), F32)
        for c in range(channels):
            window = build(c)
            corr = jnp.dot(
                units_ref[c],
                jnp.concatenate([window[:, :samples], window[:, half : half + samples]], axis=0),
                preferred_element_type=F32,
            )
            stack = stack + corr.reshape(rows // 8, 8, samples) * weights[c]
        out_ref[:rows] = stack.reshape(rows, samples).astype(BF16)
        peak = jnp.full((8, samples), -jnp.inf, F32)
        tall = rows // rounds // 8
        for r in range(rounds):
            top = jnp.max(stack[r * tall : (r + 1) * tall], axis=0)
            peak = jnp.where(held[:, r : r + 1] > 0, jnp.maximum(peak, top), peak)
        report(jnp.max(peak, axis=0, keepdims=True))


def combine(owner_ref, *refs):
    *held_refs, out_ref = refs
    rounds, block, samples = out_ref.shape
    for r in range(rounds):
        source = pick(owner_ref[...], r) ^ lax.axis_index("tm")
        for d, ref in enumerate(held_refs):

            @pl.when(source == d)
            def _():
                out_ref[r] = ref[r * block : (r + 1) * block, :]


def spec(space):
    return pl.BlockSpec(memory_space=space)


def on_device(record, templates, owner, slot, mask):
    channels, samples = record.shape
    slots, _, block, taps = templates.shape[2:]
    rounds = owner.shape[1]
    shards = lax.axis_size("tm")
    rows = rounds * block
    parts = [record] + [swap(record, "tm", d) for d in range(1, shards)]

    units = pl.pallas_call(
        prepare,
        out_shape=jax.ShapeDtypeStruct((channels, rows, taps), BF16),
        in_specs=[spec(VMEM), spec(HBM)],
        out_specs=spec(VMEM),
        scratch_shapes=[
            VMEM((rounds, channels, block, taps), BF16),
            pltpu.SemaphoreType.DMA((rounds, CHUNKS)),
        ],
        compiler_params=pltpu.CompilerParams(vmem_limit_bytes=PREPARE_VMEM),
        cost_estimate=pl.CostEstimate(flops=4 * 10**8, bytes_accessed=3 << 20, transcendentals=0),
        name="prepare",
    )(slot, templates[0, 0])

    def stack_at(flip, units, ride):
        stack = jax.ShapeDtypeStruct((rows + TAIL if ride else rows, samples), BF16)
        peak = jax.ShapeDtypeStruct((1, samples), F32)
        return pl.pallas_call(
            functools.partial(correlate, flip, shards, ride),
            out_shape=(stack,) if ride else (stack, peak),
            in_specs=[spec(VMEM)] * (shards + 3),
            out_specs=(spec(VMEM),) if ride else (spec(VMEM), spec(VMEM)),
            scratch_shapes=[
                VMEM((shards + 1, channels, samples), BF16),
                VMEM((channels, 8, samples + taps), F32),
                VMEM((channels, 8, samples), F32),
            ],
            compiler_params=pltpu.CompilerParams(vmem_limit_bytes=24 << 20),
            cost_estimate=pl.CostEstimate(
                flops=2 * rows * samples * channels * taps,
                bytes_accessed=4 << 20,
                transcendentals=0,
            ),
            name="correlate",
        )(owner, mask[None], *parts, units)

    held = {}
    for d in range(shards - 1, 1, -1):
        (piece,) = stack_at(d, units, True)
        held[d] = swap(piece, "tm", d)
        last = piece
    units, _ = lax.optimization_barrier((units, last))
    near, peak = stack_at(1, units, False)
    units, peak = lax.optimization_barrier((units, peak))
    near_peak = swap(peak, "tm", 1)
    held[0], best = stack_at(0, units, False)
    near, best = lax.optimization_barrier((near, best))
    held[1] = swap(near, "tm", 1)
    best = jnp.maximum(best, near_peak)
    for d in range(2, shards):
        best = jnp.maximum(best, held[d][rows : rows + 1].astype(F32))

    stacks = pl.pallas_call(
        combine,
        out_shape=jax.ShapeDtypeStruct((rounds, block, samples), BF16),
        in_specs=[spec(VMEM)] * (shards + 1),
        out_specs=spec(VMEM),
        compiler_params=pltpu.CompilerParams(vmem_limit_bytes=16 << 20),
        name="combine",
    )(owner, *[held[d] for d in range(shards)])

    rows_count = lax.axis_size("lib")
    step = 1
    while step < rows_count:
        flips = [step] if step == 1 or 2 * step >= rows_count else [step, 2 * step, 3 * step]
        others = [swap(best, "lib", flip) for flip in flips]
        best = functools.reduce(jnp.maximum, others, best)
        step *= 1 + len(flips)
    return stacks[None], best[0]


def solution(mesh):
    placed = (
        P(None, "tm"),
        P("lib", "tm", None, None, None, None),
        P("lib", None),
        P("lib", None),
        P(),
    )
    return jax.shard_map(
        on_device,
        mesh=mesh,
        in_specs=placed,
        out_specs=(P("lib", None, None, "tm"), P("tm")),
        check_vma=False,
    )
```

time: 39.4 us -> 30.2 us (0.77)
  Pallas kernels: 12.3 us -> 3.95 us
  starting transfers between devices: 12.5 us -> 19.9 us
  waiting for transfers between devices: 9.64 us -> 4.21 us
  local copies, waits for them, and re-layouts: 3.25 us -> 0.67 us
    pallas_call x2 -> x5, Pallas kernels: 10.3 us -> 1.78 us  [the longest x1 0.94 us: on_device(): pl.pallas_call(combine, out_shape=jax.ShapeDtypeStruct((rounds, block, sa...]
    ppermute x10 -> x11, starting transfers between devices: 12.5 us -> 19.9 us  [swap(): return lax.ppermute(x, axis, [(i, i ^ flip) for i in range(count)])]
    ppermute x10 -> x11, waiting for transfers between devices: 9.64 us -> 4.21 us  [swap(): return lax.ppermute(x, axis, [(i, i ^ flip) for i in range(count)])]
    unnamed x12 -> x8, local copies, waits for them, and re-layouts: 3.21 us -> 0.67 us
  transfers between devices with their start and end apart: 10 -> 11, of which waited for: 5 -> 4; matrix products, arithmetic and copies ran while one was open for 0% -> 0% of each run, Pallas kernels for 5% -> 12%
where the time goes in v2:
time: 30.2 us; the launch traced here: 30.1 us
  starting transfers between devices  19.9 us (66%)
  waiting for transfers between devices  4.21 us (14%)
  Pallas kernels  3.95 us (13%)
  between operations  0.73 us (2%)
  local copies, waits for them, and re-layouts  0.67 us (2%)
  other arithmetic  0.6 us (2%)
    ppermute x11, starting transfers between devices, swap(): return lax.ppermute(x, axis, [(i, i ^ flip) for i in range(count)])  19.9 us
    ppermute x11, waiting for transfers between devices, swap(): return lax.ppermute(x, axis, [(i, i ^ flip) for i in range(count)])  4.21 us
    pallas_call x1, Pallas kernels, on_device(): pl.pallas_call(prepare, out_shape=jax.ShapeDtypeStruct((channels, rows, t...  2.17 us
    pallas_call x1, Pallas kernels, on_device(): pl.pallas_call(combine, out_shape=jax.ShapeDtypeStruct((rounds, block, sa...  0.94 us
    pallas_call x4, Pallas kernels, stack_at(): pl.pallas_call(functools.partial(correlate, flip, shards, ride), out_shap...  0.83 us
    unnamed x8, local copies, waits for them, and re-layouts  0.67 us
  transfers between devices with their start and end apart: 11, of which 4 were waited for; matrix products, arithmetic and copies ran while one was open for 0% of the time, Pallas kernels for 12%

profile of v2, /device:TPU:0, one launch (start us, length us, event | category | flops | bytes accessed | tf_op | source)
XLA Modules:
  0.0 30.1 jit_solution(9438154254103891408)
XLA Ops:
  0.6 0.0 copy-start.1
  0.6 0.0 copy-start.3
  0.7 4.0 %collective-permute-start.2 = (bf16[24,512]{1,0:T(8,128)(2,1)}, bf16[24,512]{1,0:T(8,128)(2,1)S(1)}, u32[]{:S(2)}, u32[]{:S(2)}) collective-permute-start(bf16[24,512]{1,0:T(8,128)(2,1)} %refs_0_.7), channel_id=1, source_target_pairs={{0,24},{8,16},{16,8},{24,0},{1,25},{9,17},{17,9},{25,1},{2,26},{10... | collective-permute-start | bytes 73736 | tf_op jit(solution)/shard_map/ppermute | solution.py:22
  4.6 0.5 %collective-permute-start.1 = (bf16[24,512]{1,0:T(8,128)(2,1)}, bf16[24,512]{1,0:T(8,128)(2,1)S(1)}, u32[]{:S(2)}, u32[]{:S(2)}) collective-permute-start(bf16[24,512]{1,0:T(8,128)(2,1)} %refs_0_.7), channel_id=1, source_target_pairs={{0,16},{8,24},{16,0},{24,8},{1,17},{9,25},{17,1},{25,9},{2,18},{10... | collective-permute-start | bytes 73736 | tf_op jit(solution)/shard_map/ppermute | solution.py:22
  5.1 0.1 collective-permute-start
  5.3 0.0 copy-start
  5.3 0.7 %copy-done = s32[1,2]{1,0:T(1,128)S(1)} copy-done((s32[1,2]{1,0:T(1,128)S(1)}, s32[1,2]{1,0:T(1,128)}, u32[]{:S(2)}) %copy-start) | copy-done | bytes 32
  5.9 0.0 copy-start.2
  5.9 2.2 %prepare.1.refs_4_ = bf16[24,128,256]{2,1,0:T(8,128)(2,1)S(1)} custom-call(s32[1,2]{1,0:T(1,128)S(1)} %copy-done, bf16[4,24,64,256]{3,2,1,0:T(8,128)(2,1)} %bitcast.8), custom_call_target="tpu_custom_call" | custom-call | flops 400000000 | bytes 3145728 | tf_op jit(solution)/shard_map/prepare/pallas_call | solution.py:177
  8.1 0.0 collective-permute-done.2.refs_3_
  8.1 0.5 %collective-permute-done.1.refs_2_ = bf16[24,512]{1,0:T(8,128)(2,1)S(1)} collective-permute-done((bf16[24,512]{1,0:T(8,128)(2,1)}, bf16[24,512]{1,0:T(8,128)(2,1)S(1)}, u32[]{:S(2)}, u32[]{:S(2)}) %collective-permute-start.1) | collective-permute-done | bytes 24608 | tf_op jit(solution)/shard_map/ppermute | solution.py:22
  8.6 0.5 %collective-permute-done.refs_1_ = bf16[24,512]{1,0:T(8,128)(2,1)S(1)} collective-permute-done((bf16[24,512]{1,0:T(8,128)(2,1)}, bf16[24,512]{1,0:T(8,128)(2,1)S(1)}, u32[]{:S(2)}, u32[]{:S(2)}) %collective-permute-start) | collective-permute-done | bytes 24608 | tf_op jit(solution)/shard_map/ppermute | solution.py:22
  9.2 0.0 copy-done.1
  9.2 0.0 copy-done.3
  9.2 0.0 copy-done.2
  9.2 0.2 correlate.4
  9.4 1.6 %collective-permute-start.4 = (bf16[144,512]{1,0:T(8,128)(2,1)S(1)}, bf16[144,512]{1,0:T(8,128)(2,1)S(1)}, u32[]{:S(2)}, u32[]{:S(2)}) collective-permute-start(bf16[144,512]{1,0:T(8,128)(2,1)S(1)} %correlate.4), channel_id=1, source_target_pairs={{0,16},{8,24},{16,0},{24,8},{1,17},{9,25},{17,1},{25,9},{2,18},{10... | collective-permute-start | bytes 442376 | tf_op jit(solution)/shard_map/ppermute | solution.py:22
  11.0 0.2 correlate.7
  11.2 5.0 %collective-permute-start.5 = (bf16[144,512]{1,0:T(8,128)(2,1)S(1)}, bf16[144,512]{1,0:T(8,128)(2,1)S(1)}, u32[]{:S(2)}, u32[]{:S(2)}) collective-permute-start(bf16[144,512]{1,0:T(8,128)(2,1)S(1)} %correlate.7), channel_id=1, source_target_pairs={{0,24},{8,16},{16,8},{24,0},{1,25},{9,17},{17,9},{25,1},{2,26},{10... | collective-permute-start | bytes 442376 | tf_op jit(solution)/shard_map/ppermute | solution.py:22
  16.2 0.2 correlate.5
  16.4 2.2 %collective-permute-start.6 = (f32[1,512]{1,0:T(1,128)S(1)}, f32[1,512]{1,0:T(1,128)S(1)}, u32[]{:S(2)}, u32[]{:S(2)}) collective-permute-start(f32[1,512]{1,0:T(1,128)S(1)} %get-tuple-element.19), channel_id=1, source_target_pairs={{0,8},{8,0},{16,24},{24,16},{1,9},{9,1},{17,25},{25,17},{2,10},{10... | collective-permute-start | bytes 6152 | tf_op jit(solution)/shard_map/ppermute | solution.py:22
  18.6 0.2 correlate.6
  18.8 2.1 %collective-permute-start.3 = (bf16[128,512]{1,0:T(8,128)(2,1)S(1)}, bf16[128,512]{1,0:T(8,128)(2,1)S(1)}, u32[]{:S(2)}, u32[]{:S(2)}) collective-permute-start(bf16[128,512]{1,0:T(8,128)(2,1)S(1)} %get-tuple-element.17), channel_id=1, source_target_pairs={{0,8},{8,0},{16,24},{24,16},{1,9},{9,1},{17,25},{25,17},{2,10},{10... | collective-permute-start | bytes 393224 | tf_op jit(solution)/shard_map/ppermute | solution.py:22
  20.9 0.0 collective-permute-done.6
  20.9 0.0 collective-permute-done.5.refs_3_
  20.9 0.0 collective-permute-done.4.refs_2_
  20.9 0.1 collective-permute-start.7
  21.0 1.1 %collective-permute-done.7 = f32[1,512]{1,0:T(1,128)S(1)} collective-permute-done((f32[1,512]{1,0:T(1,128)S(1)}, f32[1,512]{1,0:T(1,128)S(1)}, u32[]{:S(2)}, u32[]{:S(2)}) %collective-permute-start.7) | collective-permute-done | bytes 2080 | tf_op jit(solution)/shard_map/ppermute | solution.py:22
  22.2 2.8 %collective-permute-start.10 = (f32[1,512]{1,0:T(1,128)S(1)}, f32[1,512]{1,0:T(1,128)S(1)}, u32[]{:S(2)}, u32[]{:S(2)}) collective-permute-start(f32[1,512]{1,0:T(1,128)S(1)} %max.24), channel_id=1, source_target_pairs={{0,6},{1,7},{2,4},{3,5},{4,2},{5,3},{6,0},{7,1},{8,14},{9,15},{10,... | collective-permute-start | bytes 6152 | tf_op jit(solution)/shard_map/ppermute | solution.py:22
  25.0 0.0 collective-permute-start.9
  25.0 1.5 %collective-permute-start.8 = (f32[1,512]{1,0:T(1,128)S(1)}, f32[1,512]{1,0:T(1,128)S(1)}, u32[]{:S(2)}, u32[]{:S(2)}) collective-permute-start(f32[1,512]{1,0:T(1,128)S(1)} %max.24), channel_id=1, source_target_pairs={{0,2},{1,3},{2,0},{3,1},{4,6},{5,7},{6,4},{7,5},{8,10},{9,11},{10,... | collective-permute-start | bytes 6152 | tf_op jit(solution)/shard_map/ppermute | solution.py:22
  26.5 0.0 collective-permute-done.3.refs_1_
  26.5 0.9 %combine.1 = bf16[2,64,512]{2,1,0:T(8,128)(2,1)} custom-call(s32[1,2]{1,0:T(1,128)S(1)} %copy-done.1, bf16[128,512]{1,0:T(8,128)(2,1)S(1)} %get-tuple-element.14.refs_0_, bf16[128,512]{1,0:T(8,128)(2,1)S(1)} %collective-permute-done.3.refs_1_, bf16[144,512]{1,0:T(8,128)(2,1)S(1)} %collective-permute-done.4.refs_2_, ...), custom_call_target="tpu_custom_call" | custom-call | tf_op jit(solution)/shard_map/combine/pallas_call | solution.py:229
  27.5 0.0 collective-permute-done.10
  27.5 1.9 %collective-permute-done.9 = f32[1,512]{1,0:T(1,128)S(1)} collective-permute-done((f32[1,512]{1,0:T(1,128)S(1)}, f32[1,512]{1,0:T(1,128)S(1)}, u32[]{:S(2)}, u32[]{:S(2)}) %collective-permute-start.9) | collective-permute-done | bytes 2080 | tf_op jit(solution)/shard_map/ppermute | solution.py:22
  29.5 0.0 collective-permute-done.8
  29.5 0.6 %maximum_maximum_fusion = f32[1,512]{1,0:T(1,128)} fusion(f32[1,512]{1,0:T(1,128)S(1)} %collective-permute-done.10, f32[1,512]{1,0:T(1,128)S(1)} %collective-permute-done.9, f32[1,512]{1,0:T(1,128)S(1)} %max.24, f32[1,512]{1,0:T(1,128)S(1)} %collective-permute-done.8), kind=kLoop, calls=%fused_computation.4 | loop fusion | flops 1536 | bytes 10240 | tf_op jit(solution)/shard_map/max | solution.py:243
  (2 shorter events, 0.0 us)
Async XLA Ops:
  0.6 8.5 %copy-start.1 = (s32[1,2]{1,0:T(1,128)S(1)}, s32[1,2]{1,0:T(1,128)}, u32[]{:S(2)}) copy-start(s32[1,2]{1,0:T(1,128)} %owner_ref.9) | copy-start | bytes 28
  0.6 8.5 %copy-start.3 = (s32[24]{0:T(128)S(1)}, s32[24]{0:T(128)}, u32[]{:S(2)}) copy-start(s32[24]{0:T(128)} %param.9) | copy-start | bytes 292
  0.7 7.4 %collective-permute-start.2 = (bf16[24,512]{1,0:T(8,128)(2,1)}, bf16[24,512]{1,0:T(8,128)(2,1)S(1)}, u32[]{:S(2)}, u32[]{:S(2)}) collective-permute-start(bf16[24,512]{1,0:T(8,128)(2,1)} %refs_0_.7), channel_id=1, source_target_pairs={{0,24},{8,16},{16,8},{24,0},{1,25},{9,17},{17,9},{25,1},{2,26},{10... | collective-permute-start | bytes 73736 | tf_op jit(solution)/shard_map/ppermute | solution.py:22
  4.6 4.0 %collective-permute-start.1 = (bf16[24,512]{1,0:T(8,128)(2,1)}, bf16[24,512]{1,0:T(8,128)(2,1)S(1)}, u32[]{:S(2)}, u32[]{:S(2)}) collective-permute-start(bf16[24,512]{1,0:T(8,128)(2,1)} %refs_0_.7), channel_id=1, source_target_pairs={{0,16},{8,24},{16,0},{24,8},{1,17},{9,25},{17,1},{25,9},{2,18},{10... | collective-permute-start | bytes 73736 | tf_op jit(solution)/shard_map/ppermute | solution.py:22
  5.1 4.0 %collective-permute-start = (bf16[24,512]{1,0:T(8,128)(2,1)}, bf16[24,512]{1,0:T(8,128)(2,1)S(1)}, u32[]{:S(2)}, u32[]{:S(2)}) collective-permute-start(bf16[24,512]{1,0:T(8,128)(2,1)} %refs_0_.7), channel_id=1, source_target_pairs={{0,8},{8,0},{16,24},{24,16},{1,9},{9,1},{17,25},{25,17},{2,10},{10... | collective-permute-start | bytes 73736 | tf_op jit(solution)/shard_map/ppermute | solution.py:22
  5.3 0.7 %copy-start = (s32[1,2]{1,0:T(1,128)S(1)}, s32[1,2]{1,0:T(1,128)}, u32[]{:S(2)}) copy-start(s32[1,2]{1,0:T(1,128)} %slot_ref.1) | copy-start | bytes 28
  5.9 3.3 %copy-start.2 = (bf16[24,512]{1,0:T(8,128)(2,1)S(1)}, bf16[24,512]{1,0:T(8,128)(2,1)}, u32[]{:S(2)}) copy-start(bf16[24,512]{1,0:T(8,128)(2,1)} %refs_0_.7) | copy-start | bytes 73732
  9.4 11.5 %collective-permute-start.4 = (bf16[144,512]{1,0:T(8,128)(2,1)S(1)}, bf16[144,512]{1,0:T(8,128)(2,1)S(1)}, u32[]{:S(2)}, u32[]{:S(2)}) collective-permute-start(bf16[144,512]{1,0:T(8,128)(2,1)S(1)} %correlate.4), channel_id=1, source_target_pairs={{0,16},{8,24},{16,0},{24,8},{1,17},{9,25},{17,1},{25,9},{2,18},{10... | collective-permute-start | bytes 442376 | tf_op jit(solution)/shard_map/ppermute | solution.py:22
  11.2 9.7 %collective-permute-start.5 = (bf16[144,512]{1,0:T(8,128)(2,1)S(1)}, bf16[144,512]{1,0:T(8,128)(2,1)S(1)}, u32[]{:S(2)}, u32[]{:S(2)}) collective-permute-start(bf16[144,512]{1,0:T(8,128)(2,1)S(1)} %correlate.7), channel_id=1, source_target_pairs={{0,24},{8,16},{16,8},{24,0},{1,25},{9,17},{17,9},{25,1},{2,26},{10... | collective-permute-start | bytes 442376 | tf_op jit(solution)/shard_map/ppermute | solution.py:22
  16.4 4.5 %collective-permute-start.6 = (f32[1,512]{1,0:T(1,128)S(1)}, f32[1,512]{1,0:T(1,128)S(1)}, u32[]{:S(2)}, u32[]{:S(2)}) collective-permute-start(f32[1,512]{1,0:T(1,128)S(1)} %get-tuple-element.19), channel_id=1, source_target_pairs={{0,8},{8,0},{16,24},{24,16},{1,9},{9,1},{17,25},{25,17},{2,10},{10... | collective-permute-start | bytes 6152 | tf_op jit(solution)/shard_map/ppermute | solution.py:22
  18.8 7.8 %collective-permute-start.3 = (bf16[128,512]{1,0:T(8,128)(2,1)S(1)}, bf16[128,512]{1,0:T(8,128)(2,1)S(1)}, u32[]{:S(2)}, u32[]{:S(2)}) collective-permute-start(bf16[128,512]{1,0:T(8,128)(2,1)S(1)} %get-tuple-element.17), channel_id=1, source_target_pairs={{0,8},{8,0},{16,24},{24,16},{1,9},{9,1},{17,25},{25,17},{2,10},{10... | collective-permute-start | bytes 393224 | tf_op jit(solution)/shard_map/ppermute | solution.py:22
  20.9 1.2 %collective-permute-start.7 = (f32[1,512]{1,0:T(1,128)S(1)}, f32[1,512]{1,0:T(1,128)S(1)}, u32[]{:S(2)}, u32[]{:S(2)}) collective-permute-start(f32[1,512]{1,0:T(1,128)S(1)} %fusion), channel_id=1, source_target_pairs={{0,1},{1,0},{2,3},{3,2},{4,5},{5,4},{6,7},{7,6},{8,9},{9,8},{10,11... | collective-permute-start | bytes 6152 | tf_op jit(solution)/shard_map/ppermute | solution.py:22
  22.2 5.4 %collective-permute-start.10 = (f32[1,512]{1,0:T(1,128)S(1)}, f32[1,512]{1,0:T(1,128)S(1)}, u32[]{:S(2)}, u32[]{:S(2)}) collective-permute-start(f32[1,512]{1,0:T(1,128)S(1)} %max.24), channel_id=1, source_target_pairs={{0,6},{1,7},{2,4},{3,5},{4,2},{5,3},{6,0},{7,1},{8,14},{9,15},{10,... | collective-permute-start | bytes 6152 | tf_op jit(solution)/shard_map/ppermute | solution.py:22
  25.0 4.5 %collective-permute-start.9 = (f32[1,512]{1,0:T(1,128)S(1)}, f32[1,512]{1,0:T(1,128)S(1)}, u32[]{:S(2)}, u32[]{:S(2)}) collective-permute-start(f32[1,512]{1,0:T(1,128)S(1)} %max.24), channel_id=1, source_target_pairs={{0,4},{1,5},{2,6},{3,7},{4,0},{5,1},{6,2},{7,3},{8,12},{9,13},{10,... | collective-permute-start | bytes 6152 | tf_op jit(solution)/shard_map/ppermute | solution.py:22
  25.0 4.5 %collective-permute-start.8 = (f32[1,512]{1,0:T(1,128)S(1)}, f32[1,512]{1,0:T(1,128)S(1)}, u32[]{:S(2)}, u32[]{:S(2)}) collective-permute-start(f32[1,512]{1,0:T(1,128)S(1)} %max.24), channel_id=1, source_target_pairs={{0,2},{1,3},{2,0},{3,1},{4,6},{5,7},{6,4},{7,5},{8,10},{9,11},{10,... | collective-permute-start | bytes 6152 | tf_op jit(solution)/shard_map/ppermute | solution.py:22

commit v3 on v2

--- a/solution.py
+++ b/solution.py
@@ -69,8 +69,8 @@
                     ).astype(BF16)
 
 
-def correlate(flip, shards, ride, owner_ref, mask_ref, *refs):
-    part_refs, refs = refs[:shards], refs[shards:]
+def correlate(flip, near, shards, ride, owner_ref, mask_ref, *refs):
+    part_refs, refs = refs[: len(near)], refs[len(near) :]
     units_ref, out_ref, *refs = refs
     peak_ref = None if ride else refs.pop(0)
     spans, lines, weights = refs
@@ -97,8 +97,8 @@
     @pl.when(mine)
     def _():
         spans[shards] = jnp.zeros((channels, samples), BF16)
-        for d in range(shards):
-            spans[me ^ d] = part_refs[d][...]
+        for d, part_ref in zip(near, part_refs):
+            spans[me ^ d] = part_ref[...]
         row = lax.broadcasted_iota(jnp.int32, (channels, channels), 0)
         col = lax.broadcasted_iota(jnp.int32, (channels, channels), 1)
         live = jnp.where(row == col, jnp.broadcast_to(mask_ref[...], row.shape), 0)
@@ -189,12 +189,15 @@
     )(slot, templates[0, 0])
 
     def stack_at(flip, units, ride):
+        near = [flip]
+        while len(near) <= (shards - 1).bit_length():
+            near.append(flip ^ ((1 << len(near)) - 1))
         stack = jax.ShapeDtypeStruct((rows + TAIL if ride else rows, samples), BF16)
         peak = jax.ShapeDtypeStruct((1, samples), F32)
         return pl.pallas_call(
-            functools.partial(correlate, flip, shards, ride),
+            functools.partial(correlate, flip, near, shards, ride),
             out_shape=(stack,) if ride else (stack, peak),
-            in_specs=[spec(VMEM)] * (shards + 3),
+            in_specs=[spec(VMEM)] * (len(near) + 3),
             out_specs=(spec(VMEM),) if ride else (spec(VMEM), spec(VMEM)),
             scratch_shapes=[
                 VMEM((shards + 1, channels, samples), BF16),
@@ -208,22 +211,22 @@
                 transcendentals=0,
             ),
             name="correlate",
-        )(owner, mask[None], *parts, units)
-
+        )(owner, mask[None], *[parts[d] for d in near], units)
+
+    *early, late = [1, 3, *range(4, shards), 2]
     held = {}
-    for d in range(shards - 1, 1, -1):
-        (piece,) = stack_at(d, units, True)
-        held[d] = swap(piece, "tm", d)
-        last = piece
+    for d in early:
+        (last,) = stack_at(d, units, True)
+        held[d] = swap(last, "tm", d)
     units, _ = lax.optimization_barrier((units, last))
-    near, peak = stack_at(1, units, False)
+    near, peak = stack_at(late, units, False)
     units, peak = lax.optimization_barrier((units, peak))
-    near_peak = swap(peak, "tm", 1)
+    near_peak = swap(peak, "tm", late)
     held[0], best = stack_at(0, units, False)
     near, best = lax.optimization_barrier((near, best))
-    held[1] = swap(near, "tm", 1)
+    held[late] = swap(near, "tm", late)
     best = jnp.maximum(best, near_peak)
-    for d in range(2, shards):
+    for d in early:
         best = jnp.maximum(best, held[d][rows : rows + 1].astype(F32))
 
     stacks = pl.pallas_call(

time: 30.2 us -> 31.1 us (1.030); the launches traced: 30.1 us -> 30.6 us
  starting transfers between devices: 19.9 us -> 20.4 us
    ppermute x11, starting transfers between devices: 19.9 us -> 20.4 us  [swap(): return lax.ppermute(x, axis, [(i, i ^ flip) for i in range(count)])]
  transfers between devices with their start and end apart: 11 -> 11, of which waited for: 4 -> 3; matrix products, arithmetic and copies ran while one was open for 0% -> 0% of each run, Pallas kernels for 12% -> 12%
where the time goes in v3:
time: 31.1 us; the launch traced here: 30.6 us
  starting transfers between devices  20.4 us (66%)
  waiting for transfers between devices  4.44 us (14%)
  Pallas kernels  3.8 us (12%)
  between operations  0.73 us (2%)
  local copies, waits for them, and re-layouts  0.67 us (2%)
  other arithmetic  0.6 us (2%)
    ppermute x11, starting transfers between devices, swap(): return lax.ppermute(x, axis, [(i, i ^ flip) for i in range(count)])  20.4 us
    ppermute x11, waiting for transfers between devices, swap(): return lax.ppermute(x, axis, [(i, i ^ flip) for i in range(count)])  4.44 us
    pallas_call x1, Pallas kernels, on_device(): pl.pallas_call(prepare, out_shape=jax.ShapeDtypeStruct((channels, rows, t...  2.02 us
    pallas_call x1, Pallas kernels, on_device(): pl.pallas_call(combine, out_shape=jax.ShapeDtypeStruct((rounds, block, sa...  0.94 us
    pallas_call x4, Pallas kernels, stack_at(): pl.pallas_call(functools.partial(correlate, flip, near, shards, ride), ou...  0.83 us
    unnamed x8, local copies, waits for them, and re-layouts  0.67 us
  transfers between devices with their start and end apart: 11, of which 3 were waited for; matrix products, arithmetic and copies ran while one was open for 0% of the time, Pallas kernels for 12%

profile of v3, /device:TPU:0, one launch (start us, length us, event | category | flops | bytes accessed | tf_op | source)
XLA Modules:
  0.0 30.6 jit_solution(6340797873806137912)
XLA Ops:
  0.6 0.0 copy-start.1
  0.6 0.0 copy-start.3
  0.7 3.0 %collective-permute-start.2 = (bf16[24,512]{1,0:T(8,128)(2,1)}, bf16[24,512]{1,0:T(8,128)(2,1)S(1)}, u32[]{:S(2)}, u32[]{:S(2)}) collective-permute-start(bf16[24,512]{1,0:T(8,128)(2,1)} %refs_1_.1), channel_id=1, source_target_pairs={{0,16},{8,24},{16,0},{24,8},{1,17},{9,25},{17,1},{25,9},{2,18},{10... | collective-permute-start | bytes 73736 | tf_op jit(solution)/shard_map/ppermute | solution.py:22
  3.7 1.4 %collective-permute-start.1 = (bf16[24,512]{1,0:T(8,128)(2,1)}, bf16[24,512]{1,0:T(8,128)(2,1)S(1)}, u32[]{:S(2)}, u32[]{:S(2)}) collective-permute-start(bf16[24,512]{1,0:T(8,128)(2,1)} %refs_1_.1), channel_id=1, source_target_pairs={{0,24},{8,16},{16,8},{24,0},{1,25},{9,17},{17,9},{25,1},{2,26},{10... | collective-permute-start | bytes 73736 | tf_op jit(solution)/shard_map/ppermute | solution.py:22
  5.1 0.1 collective-permute-start
  5.2 0.0 copy-start
  5.2 0.7 %copy-done = s32[1,2]{1,0:T(1,128)S(1)} copy-done((s32[1,2]{1,0:T(1,128)S(1)}, s32[1,2]{1,0:T(1,128)}, u32[]{:S(2)}) %copy-start) | copy-done | bytes 32
  5.9 0.0 copy-start.2
  5.9 2.0 %prepare.1.refs_3_ = bf16[24,128,256]{2,1,0:T(8,128)(2,1)S(1)} custom-call(s32[1,2]{1,0:T(1,128)S(1)} %copy-done, bf16[4,24,64,256]{3,2,1,0:T(8,128)(2,1)} %bitcast.8), custom_call_target="tpu_custom_call" | custom-call | flops 400000000 | bytes 3145728 | tf_op jit(solution)/shard_map/prepare/pallas_call | solution.py:177
  7.9 0.0 collective-permute-done.2.refs_1_.refs_0_.refs_2_
  7.9 0.8 %collective-permute-done.1.refs_0_.refs_1_.refs_2_ = bf16[24,512]{1,0:T(8,128)(2,1)S(1)} collective-permute-done((bf16[24,512]{1,0:T(8,128)(2,1)}, bf16[24,512]{1,0:T(8,128)(2,1)S(1)}, u32[]{:S(2)}, u32[]{:S(2)}) %collective-permute-start.1) | collective-permute-done | bytes 24608 | tf_op jit(solution)/shard_map/ppermute | solution.py:22
  8.7 0.0 copy-done.1
  8.7 0.0 copy-done.3
  8.7 0.0 copy-done.2
  8.7 0.2 correlate.4
  8.9 2.2 %collective-permute-start.5 = (bf16[144,512]{1,0:T(8,128)(2,1)S(1)}, bf16[144,512]{1,0:T(8,128)(2,1)S(1)}, u32[]{:S(2)}, u32[]{:S(2)}) collective-permute-start(bf16[144,512]{1,0:T(8,128)(2,1)S(1)} %correlate.4), channel_id=1, source_target_pairs={{0,24},{8,16},{16,8},{24,0},{1,25},{9,17},{17,9},{25,1},{2,26},{10... | collective-permute-start | bytes 442376 | tf_op jit(solution)/shard_map/ppermute | solution.py:22
  11.1 0.0 collective-permute-done.refs_2_.refs_1_.refs_0_
  11.1 0.2 correlate.7
  11.4 4.7 %collective-permute-start.3 = (bf16[144,512]{1,0:T(8,128)(2,1)S(1)}, bf16[144,512]{1,0:T(8,128)(2,1)S(1)}, u32[]{:S(2)}, u32[]{:S(2)}) collective-permute-start(bf16[144,512]{1,0:T(8,128)(2,1)S(1)} %correlate.7), channel_id=1, source_target_pairs={{0,8},{8,0},{16,24},{24,16},{1,9},{9,1},{17,25},{25,17},{2,10},{10... | collective-permute-start | bytes 442376 | tf_op jit(solution)/shard_map/ppermute | solution.py:22
  16.0 0.2 correlate.5
  16.2 2.3 %collective-permute-start.6 = (f32[1,512]{1,0:T(1,128)S(1)}, f32[1,512]{1,0:T(1,128)S(1)}, u32[]{:S(2)}, u32[]{:S(2)}) collective-permute-start(f32[1,512]{1,0:T(1,128)S(1)} %get-tuple-element.19), channel_id=1, source_target_pairs={{0,16},{8,24},{16,0},{24,8},{1,17},{9,25},{17,1},{25,9},{2,18},{10... | collective-permute-start | bytes 6152 | tf_op jit(solution)/shard_map/ppermute | solution.py:22
  18.6 0.2 correlate.6
  18.8 2.1 %collective-permute-start.4 = (bf16[128,512]{1,0:T(8,128)(2,1)S(1)}, bf16[128,512]{1,0:T(8,128)(2,1)S(1)}, u32[]{:S(2)}, u32[]{:S(2)}) collective-permute-start(bf16[128,512]{1,0:T(8,128)(2,1)S(1)} %get-tuple-element.17), channel_id=1, source_target_pairs={{0,16},{8,24},{16,0},{24,8},{1,17},{9,25},{17,1},{25,9},{2,18},{10... | collective-permute-start | bytes 393224 | tf_op jit(solution)/shard_map/ppermute | solution.py:22
  20.9 0.0 collective-permute-done.6
  20.9 0.0 collective-permute-done.3.refs_1_
  20.9 0.0 collective-permute-done.5.refs_3_
  20.9 0.1 collective-permute-start.7
  21.0 1.1 %collective-permute-done.7 = f32[1,512]{1,0:T(1,128)S(1)} collective-permute-done((f32[1,512]{1,0:T(1,128)S(1)}, f32[1,512]{1,0:T(1,128)S(1)}, u32[]{:S(2)}, u32[]{:S(2)}) %collective-permute-start.7) | collective-permute-done | bytes 2080 | tf_op jit(solution)/shard_map/ppermute | solution.py:22
  22.2 3.4 %collective-permute-start.10 = (f32[1,512]{1,0:T(1,128)S(1)}, f32[1,512]{1,0:T(1,128)S(1)}, u32[]{:S(2)}, u32[]{:S(2)}) collective-permute-start(f32[1,512]{1,0:T(1,128)S(1)} %max.24), channel_id=1, source_target_pairs={{0,6},{1,7},{2,4},{3,5},{4,2},{5,3},{6,0},{7,1},{8,14},{9,15},{10,... | collective-permute-start | bytes 6152 | tf_op jit(solution)/shard_map/ppermute | solution.py:22
  25.5 0.0 collective-permute-start.9
  25.5 1.0 %collective-permute-start.8 = (f32[1,512]{1,0:T(1,128)S(1)}, f32[1,512]{1,0:T(1,128)S(1)}, u32[]{:S(2)}, u32[]{:S(2)}) collective-permute-start(f32[1,512]{1,0:T(1,128)S(1)} %max.24), channel_id=1, source_target_pairs={{0,2},{1,3},{2,0},{3,1},{4,6},{5,7},{6,4},{7,5},{8,10},{9,11},{10,... | collective-permute-start | bytes 6152 | tf_op jit(solution)/shard_map/ppermute | solution.py:22
  26.6 0.0 collective-permute-done.4.refs_2_
  26.6 0.9 %combine.1 = bf16[2,64,512]{2,1,0:T(8,128)(2,1)} custom-call(s32[1,2]{1,0:T(1,128)S(1)} %copy-done.1, bf16[128,512]{1,0:T(8,128)(2,1)S(1)} %get-tuple-element.14.refs_0_, bf16[144,512]{1,0:T(8,128)(2,1)S(1)} %collective-permute-done.3.refs_1_, bf16[128,512]{1,0:T(8,128)(2,1)S(1)} %collective-permute-done.4.refs_2_, ...), custom_call_target="tpu_custom_call" | custom-call | tf_op jit(solution)/shard_map/combine/pallas_call | solution.py:232
  27.5 0.0 collective-permute-done.10
  27.6 2.5 %collective-permute-done.9 = f32[1,512]{1,0:T(1,128)S(1)} collective-permute-done((f32[1,512]{1,0:T(1,128)S(1)}, f32[1,512]{1,0:T(1,128)S(1)}, u32[]{:S(2)}, u32[]{:S(2)}) %collective-permute-start.9) | collective-permute-done | bytes 2080 | tf_op jit(solution)/shard_map/ppermute | solution.py:22
  30.0 0.0 collective-permute-done.8
  30.0 0.6 %maximum_maximum_fusion = f32[1,512]{1,0:T(1,128)} fusion(f32[1,512]{1,0:T(1,128)S(1)} %collective-permute-done.10, f32[1,512]{1,0:T(1,128)S(1)} %collective-permute-done.9, f32[1,512]{1,0:T(1,128)S(1)} %max.24, f32[1,512]{1,0:T(1,128)S(1)} %collective-permute-done.8), kind=kLoop, calls=%fused_computation.4 | loop fusion | flops 1536 | bytes 10240 | tf_op jit(solution)/shard_map/max | solution.py:246
  (2 shorter events, 0.0 us)
Async XLA Ops:
  0.6 8.1 %copy-start.1 = (s32[1,2]{1,0:T(1,128)S(1)}, s32[1,2]{1,0:T(1,128)}, u32[]{:S(2)}) copy-start(s32[1,2]{1,0:T(1,128)} %owner_ref.9) | copy-start | bytes 28
  0.6 8.0 %copy-start.3 = (s32[24]{0:T(128)S(1)}, s32[24]{0:T(128)}, u32[]{:S(2)}) copy-start(s32[24]{0:T(128)} %param.9) | copy-start | bytes 292
  0.7 7.3 %collective-permute-start.2 = (bf16[24,512]{1,0:T(8,128)(2,1)}, bf16[24,512]{1,0:T(8,128)(2,1)S(1)}, u32[]{:S(2)}, u32[]{:S(2)}) collective-permute-start(bf16[24,512]{1,0:T(8,128)(2,1)} %refs_1_.1), channel_id=1, source_target_pairs={{0,16},{8,24},{16,0},{24,8},{1,17},{9,25},{17,1},{25,9},{2,18},{10... | collective-permute-start | bytes 73736 | tf_op jit(solution)/shard_map/ppermute | solution.py:22
  3.7 5.0 %collective-permute-start.1 = (bf16[24,512]{1,0:T(8,128)(2,1)}, bf16[24,512]{1,0:T(8,128)(2,1)S(1)}, u32[]{:S(2)}, u32[]{:S(2)}) collective-permute-start(bf16[24,512]{1,0:T(8,128)(2,1)} %refs_1_.1), channel_id=1, source_target_pairs={{0,24},{8,16},{16,8},{24,0},{1,25},{9,17},{17,9},{25,1},{2,26},{10... | collective-permute-start | bytes 73736 | tf_op jit(solution)/shard_map/ppermute | solution.py:22
  5.1 6.0 %collective-permute-start = (bf16[24,512]{1,0:T(8,128)(2,1)}, bf16[24,512]{1,0:T(8,128)(2,1)S(1)}, u32[]{:S(2)}, u32[]{:S(2)}) collective-permute-start(bf16[24,512]{1,0:T(8,128)(2,1)} %refs_1_.1), channel_id=1, source_target_pairs={{0,8},{8,0},{16,24},{24,16},{1,9},{9,1},{17,25},{25,17},{2,10},{10... | collective-permute-start | bytes 73736 | tf_op jit(solution)/shard_map/ppermute | solution.py:22
  5.2 0.7 %copy-start = (s32[1,2]{1,0:T(1,128)S(1)}, s32[1,2]{1,0:T(1,128)}, u32[]{:S(2)}) copy-start(s32[1,2]{1,0:T(1,128)} %slot_ref.1) | copy-start | bytes 28
  5.9 2.8 %copy-start.2 = (bf16[24,512]{1,0:T(8,128)(2,1)S(1)}, bf16[24,512]{1,0:T(8,128)(2,1)}, u32[]{:S(2)}) copy-start(bf16[24,512]{1,0:T(8,128)(2,1)} %refs_1_.1) | copy-start | bytes 73732
  8.9 12.0 %collective-permute-start.5 = (bf16[144,512]{1,0:T(8,128)(2,1)S(1)}, bf16[144,512]{1,0:T(8,128)(2,1)S(1)}, u32[]{:S(2)}, u32[]{:S(2)}) collective-permute-start(bf16[144,512]{1,0:T(8,128)(2,1)S(1)} %correlate.4), channel_id=1, source_target_pairs={{0,24},{8,16},{16,8},{24,0},{1,25},{9,17},{17,9},{25,1},{2,26},{10... | collective-permute-start | bytes 442376 | tf_op jit(solution)/shard_map/ppermute | solution.py:22
  11.4 9.6 %collective-permute-start.3 = (bf16[144,512]{1,0:T(8,128)(2,1)S(1)}, bf16[144,512]{1,0:T(8,128)(2,1)S(1)}, u32[]{:S(2)}, u32[]{:S(2)}) collective-permute-start(bf16[144,512]{1,0:T(8,128)(2,1)S(1)} %correlate.7), channel_id=1, source_target_pairs={{0,8},{8,0},{16,24},{24,16},{1,9},{9,1},{17,25},{25,17},{2,10},{10... | collective-permute-start | bytes 442376 | tf_op jit(solution)/shard_map/ppermute | solution.py:22
  16.2 4.7 %collective-permute-start.6 = (f32[1,512]{1,0:T(1,128)S(1)}, f32[1,512]{1,0:T(1,128)S(1)}, u32[]{:S(2)}, u32[]{:S(2)}) collective-permute-start(f32[1,512]{1,0:T(1,128)S(1)} %get-tuple-element.19), channel_id=1, source_target_pairs={{0,16},{8,24},{16,0},{24,8},{1,17},{9,25},{17,1},{25,9},{2,18},{10... | collective-permute-start | bytes 6152 | tf_op jit(solution)/shard_map/ppermute | solution.py:22
  18.8 7.8 %collective-permute-start.4 = (bf16[128,512]{1,0:T(8,128)(2,1)S(1)}, bf16[128,512]{1,0:T(8,128)(2,1)S(1)}, u32[]{:S(2)}, u32[]{:S(2)}) collective-permute-start(bf16[128,512]{1,0:T(8,128)(2,1)S(1)} %get-tuple-element.17), channel_id=1, source_target_pairs={{0,16},{8,24},{16,0},{24,8},{1,17},{9,25},{17,1},{25,9},{2,18},{10... | collective-permute-start | bytes 393224 | tf_op jit(solution)/shard_map/ppermute | solution.py:22
  20.9 1.2 %collective-permute-start.7 = (f32[1,512]{1,0:T(1,128)S(1)}, f32[1,512]{1,0:T(1,128)S(1)}, u32[]{:S(2)}, u32[]{:S(2)}) collective-permute-start(f32[1,512]{1,0:T(1,128)S(1)} %fusion), channel_id=1, source_target_pairs={{0,1},{1,0},{2,3},{3,2},{4,5},{5,4},{6,7},{7,6},{8,9},{9,8},{10,11... | collective-permute-start | bytes 6152 | tf_op jit(solution)/shard_map/ppermute | solution.py:22
  22.2 5.4 %collective-permute-start.10 = (f32[1,512]{1,0:T(1,128)S(1)}, f32[1,512]{1,0:T(1,128)S(1)}, u32[]{:S(2)}, u32[]{:S(2)}) collective-permute-start(f32[1,512]{1,0:T(1,128)S(1)} %max.24), channel_id=1, source_target_pairs={{0,6},{1,7},{2,4},{3,5},{4,2},{5,3},{6,0},{7,1},{8,14},{9,15},{10,... | collective-permute-start | bytes 6152 | tf_op jit(solution)/shard_map/ppermute | solution.py:22
  25.5 4.5 %collective-permute-start.9 = (f32[1,512]{1,0:T(1,128)S(1)}, f32[1,512]{1,0:T(1,128)S(1)}, u32[]{:S(2)}, u32[]{:S(2)}) collective-permute-start(f32[1,512]{1,0:T(1,128)S(1)} %max.24), channel_id=1, source_target_pairs={{0,4},{1,5},{2,6},{3,7},{4,0},{5,1},{6,2},{7,3},{8,12},{9,13},{10,... | collective-permute-start | bytes 6152 | tf_op jit(solution)/shard_map/ppermute | solution.py:22
  25.5 4.5 %collective-permute-start.8 = (f32[1,512]{1,0:T(1,128)S(1)}, f32[1,512]{1,0:T(1,128)S(1)}, u32[]{:S(2)}, u32[]{:S(2)}) collective-permute-start(f32[1,512]{1,0:T(1,128)S(1)} %max.24), channel_id=1, source_target_pairs={{0,2},{1,3},{2,0},{3,1},{4,6},{5,7},{6,4},{7,5},{8,10},{9,11},{10,... | collective-permute-start | bytes 6152 | tf_op jit(solution)/shard_map/ppermute | solution.py:22

commit v4 on v3

--- a/solution.py
+++ b/solution.py
@@ -153,13 +153,13 @@
 def combine(owner_ref, *refs):
     *held_refs, out_ref = refs
     rounds, block, samples = out_ref.shape
+    me = lax.axis_index("tm")
     for r in range(rounds):
-        source = pick(owner_ref[...], r) ^ lax.axis_index("tm")
-        for d, ref in enumerate(held_refs):
-
-            @pl.when(source == d)
-            def _():
-                out_ref[r] = ref[r * block : (r + 1) * block, :]
+        source = pick(owner_ref[...], r) ^ me
+        taken = held_refs[0][r * block : (r + 1) * block, :]
+        for d in range(1, len(held_refs)):
+            taken = jnp.where(source == d, held_refs[d][r * block : (r + 1) * block, :], taken)
+        out_ref[r] = taken
 
 
 def spec(space):

time: 31.1 us -> 31.4 us (level); the launches traced: 30.6 us -> 31.6 us
  starting transfers between devices: 20.4 us -> 11.5 us
  Pallas kernels: 3.8 us -> 11.8 us
  waiting for transfers between devices: 4.44 us -> 6.17 us
    ppermute x11, starting transfers between devices: 20.4 us -> 11.5 us  [swap(): return lax.ppermute(x, axis, [(i, i ^ flip) for i in range(count)])]
    pallas_call x4, Pallas kernels: 0.83 us -> 9.01 us  [stack_at(): pl.pallas_call(functools.partial(correlate, flip, near, shards, ride), ou...]
    ppermute x11, waiting for transfers between devices: 4.44 us -> 6.17 us  [swap(): return lax.ppermute(x, axis, [(i, i ^ flip) for i in range(count)])]
  transfers between devices with their start and end apart: 11 -> 11, of which waited for: 3 -> 5; matrix products, arithmetic and copies ran while one was open for 0% -> 0% of each run, Pallas kernels for 12% -> 37%
where the time goes in v4:
time: 31.4 us; the launch traced here: 31.6 us
  Pallas kernels  11.8 us (38%)
  starting transfers between devices  11.5 us (37%)
  waiting for transfers between devices  6.17 us (20%)
  between operations  0.74 us (2%)
  local copies, waits for them, and re-layouts  0.67 us (2%)
  other arithmetic  0.6 us (2%)
    ppermute x11, starting transfers between devices, swap(): return lax.ppermute(x, axis, [(i, i ^ flip) for i in range(count)])  11.5 us
    pallas_call x4, Pallas kernels, stack_at(): pl.pallas_call(functools.partial(correlate, flip, near, shards, ride), ou...  9.01 us
    ppermute x11, waiting for transfers between devices, swap(): return lax.ppermute(x, axis, [(i, i ^ flip) for i in range(count)])  6.17 us
    pallas_call x1, Pallas kernels, on_device(): pl.pallas_call(prepare, out_shape=jax.ShapeDtypeStruct((channels, rows, t...  2.02 us
    pallas_call x1, Pallas kernels, on_device(): pl.pallas_call(combine, out_shape=jax.ShapeDtypeStruct((rounds, block, sa...  0.8 us
    unnamed x8, local copies, waits for them, and re-layouts  0.67 us
  transfers between devices with their start and end apart: 11, of which 5 were waited for; matrix products, arithmetic and copies ran while one was open for 0% of the time, Pallas kernels for 37%

profile of v4, /device:TPU:0, one launch (start us, length us, event | category | flops | bytes accessed | tf_op | source)
XLA Modules:
  0.0 31.6 jit_solution(7294253533762703680)
XLA Ops:
  0.6 0.0 copy-start.1
  0.6 0.0 copy-start.3
  0.7 3.0 %collective-permute-start.2 = (bf16[24,512]{1,0:T(8,128)(2,1)}, bf16[24,512]{1,0:T(8,128)(2,1)S(1)}, u32[]{:S(2)}, u32[]{:S(2)}) collective-permute-start(bf16[24,512]{1,0:T(8,128)(2,1)} %refs_1_.1), channel_id=1, source_target_pairs={{0,16},{8,24},{16,0},{24,8},{1,17},{9,25},{17,1},{25,9},{2,18},{10... | collective-permute-start | bytes 73736 | tf_op jit(solution)/shard_map/ppermute | solution.py:22
  3.7 1.4 %collective-permute-start.1 = (bf16[24,512]{1,0:T(8,128)(2,1)}, bf16[24,512]{1,0:T(8,128)(2,1)S(1)}, u32[]{:S(2)}, u32[]{:S(2)}) collective-permute-start(bf16[24,512]{1,0:T(8,128)(2,1)} %refs_1_.1), channel_id=1, source_target_pairs={{0,24},{8,16},{16,8},{24,0},{1,25},{9,17},{17,9},{25,1},{2,26},{10... | collective-permute-start | bytes 73736 | tf_op jit(solution)/shard_map/ppermute | solution.py:22
  5.1 0.1 collective-permute-start
  5.2 0.0 copy-start
  5.2 0.7 %copy-done = s32[1,2]{1,0:T(1,128)S(1)} copy-done((s32[1,2]{1,0:T(1,128)S(1)}, s32[1,2]{1,0:T(1,128)}, u32[]{:S(2)}) %copy-start) | copy-done | bytes 32
  5.9 0.0 copy-start.2
  5.9 2.0 %prepare.1.refs_3_ = bf16[24,128,256]{2,1,0:T(8,128)(2,1)S(1)} custom-call(s32[1,2]{1,0:T(1,128)S(1)} %copy-done, bf16[4,24,64,256]{3,2,1,0:T(8,128)(2,1)} %bitcast.8), custom_call_target="tpu_custom_call" | custom-call | flops 400000000 | bytes 3145728 | tf_op jit(solution)/shard_map/prepare/pallas_call | solution.py:177
  7.9 0.0 collective-permute-done.2.refs_1_.refs_0_.refs_2_
  7.9 0.8 %collective-permute-done.1.refs_0_.refs_1_.refs_2_ = bf16[24,512]{1,0:T(8,128)(2,1)S(1)} collective-permute-done((bf16[24,512]{1,0:T(8,128)(2,1)}, bf16[24,512]{1,0:T(8,128)(2,1)S(1)}, u32[]{:S(2)}, u32[]{:S(2)}) %collective-permute-start.1) | collective-permute-done | bytes 24608 | tf_op jit(solution)/shard_map/ppermute | solution.py:22
  8.7 0.0 copy-done.1
  8.7 0.0 copy-done.3
  8.7 0.0 copy-done.2
  8.7 2.3 %correlate.4 = bf16[144,512]{1,0:T(8,128)(2,1)S(1)} custom-call(s32[1,2]{1,0:T(1,128)S(1)} %copy-done.1, s32[1,24]{1,0:T(1,128)S(1)} %bitcast.4, bf16[24,512]{1,0:T(8,128)(2,1)S(1)} %collective-permute-done.1.refs_0_.refs_1_.refs_2_, bf16[24,512]{1,0:T(8,128)(2,1)S(1)} %collective-permute-done.2.refs_1_.refs_0_.refs_2_, bf16[24,512]{1,0:T(8,128)(2,1)S(1)} %copy-done.2, ...), custom_call_target="tpu_custom_call" | custom-call | flops 805306368 | bytes 4194304 | tf_op jit(solution)/shard_map/correlate/pallas_call | solution.py:197
  11.0 0.2 collective-permute-start.5
  11.1 0.0 collective-permute-done.refs_2_.refs_1_.refs_0_
  11.1 2.2 %correlate.7 = bf16[144,512]{1,0:T(8,128)(2,1)S(1)} custom-call(s32[1,2]{1,0:T(1,128)S(1)} %copy-done.1, s32[1,24]{1,0:T(1,128)S(1)} %bitcast.5, bf16[24,512]{1,0:T(8,128)(2,1)S(1)} %collective-permute-done.refs_2_.refs_1_.refs_0_, bf16[24,512]{1,0:T(8,128)(2,1)S(1)} %copy-done.2, bf16[24,512]{1,0:T(8,128)(2,1)S(1)} %collective-permute-done.2.refs_1_.refs_0_.refs_2_, ...), custom_call_target="tpu_custom_call" | custom-call | flops 805306368 | bytes 4194304 | tf_op jit(solution)/shard_map/correlate/pallas_call | solution.py:197
  13.4 1.4 %collective-permute-start.3 = (bf16[144,512]{1,0:T(8,128)(2,1)S(1)}, bf16[144,512]{1,0:T(8,128)(2,1)S(1)}, u32[]{:S(2)}, u32[]{:S(2)}) collective-permute-start(bf16[144,512]{1,0:T(8,128)(2,1)S(1)} %correlate.7), channel_id=1, source_target_pairs={{0,8},{8,0},{16,24},{24,16},{1,9},{9,1},{17,25},{25,17},{2,10},{10... | collective-permute-start | bytes 442376 | tf_op jit(solution)/shard_map/ppermute | solution.py:22
  14.8 2.2 %correlate.5 = (bf16[128,512]{1,0:T(8,128)(2,1)S(1)}, f32[1,512]{1,0:T(1,128)S(1)}) custom-call(s32[1,2]{1,0:T(1,128)S(1)} %copy-done.1, s32[1,24]{1,0:T(1,128)S(1)} %bitcast.6, bf16[24,512]{1,0:T(8,128)(2,1)S(1)} %collective-permute-done.2.refs_1_.refs_0_.refs_2_, bf16[24,512]{1,0:T(8,128)(2,1)S(1)} %collective-permute-done.1.refs_0_.refs_1_.refs_2_, ...), custom_call_target="tpu_custom_call" | custom-call | flops 805306368 | bytes 4194304 | tf_op jit(solution)/shard_map/correlate/pallas_call | solution.py:197
  17.0 0.1 collective-permute-start.6
  17.1 2.3 %correlate.6 = (bf16[128,512]{1,0:T(8,128)(2,1)S(1)}, f32[1,512]{1,0:T(1,128)S(1)}) custom-call(s32[1,2]{1,0:T(1,128)S(1)} %copy-done.1, s32[1,24]{1,0:T(1,128)S(1)} %bitcast.7, bf16[24,512]{1,0:T(8,128)(2,1)S(1)} %copy-done.2, bf16[24,512]{1,0:T(8,128)(2,1)S(1)} %collective-permute-done.refs_2_.refs_1_.refs_0_, ...), custom_call_target="tpu_custom_call" | custom-call | flops 805306368 | bytes 4194304 | tf_op jit(solution)/shard_map/correlate/pallas_call | solution.py:197
  19.4 0.1 collective-permute-start.4
  19.5 1.2 %collective-permute-done.6 = f32[1,512]{1,0:T(1,128)S(1)} collective-permute-done((f32[1,512]{1,0:T(1,128)S(1)}, f32[1,512]{1,0:T(1,128)S(1)}, u32[]{:S(2)}, u32[]{:S(2)}) %collective-permute-start.6) | collective-permute-done | bytes 2080 | tf_op jit(solution)/shard_map/ppermute | solution.py:22
  20.7 0.0 collective-permute-done.3.refs_1_
  20.7 0.0 collective-permute-done.5.refs_3_
  20.7 0.1 collective-permute-start.7
  20.8 1.1 %collective-permute-done.7 = f32[1,512]{1,0:T(1,128)S(1)} collective-permute-done((f32[1,512]{1,0:T(1,128)S(1)}, f32[1,512]{1,0:T(1,128)S(1)}, u32[]{:S(2)}, u32[]{:S(2)}) %collective-permute-start.7) | collective-permute-done | bytes 2080 | tf_op jit(solution)/shard_map/ppermute | solution.py:22
  21.9 4.5 %collective-permute-start.10 = (f32[1,512]{1,0:T(1,128)S(1)}, f32[1,512]{1,0:T(1,128)S(1)}, u32[]{:S(2)}, u32[]{:S(2)}) collective-permute-start(f32[1,512]{1,0:T(1,128)S(1)} %max.24), channel_id=1, source_target_pairs={{0,6},{1,7},{2,4},{3,5},{4,2},{5,3},{6,0},{7,1},{8,14},{9,15},{10,... | collective-permute-start | bytes 6152 | tf_op jit(solution)/shard_map/ppermute | solution.py:22
  26.5 0.0 collective-permute-start.9
  26.5 0.6 %collective-permute-start.8 = (f32[1,512]{1,0:T(1,128)S(1)}, f32[1,512]{1,0:T(1,128)S(1)}, u32[]{:S(2)}, u32[]{:S(2)}) collective-permute-start(f32[1,512]{1,0:T(1,128)S(1)} %max.24), channel_id=1, source_target_pairs={{0,2},{1,3},{2,0},{3,1},{4,6},{5,7},{6,4},{7,5},{8,10},{9,11},{10,... | collective-permute-start | bytes 6152 | tf_op jit(solution)/shard_map/ppermute | solution.py:22
  27.1 0.0 collective-permute-done.4.refs_2_
  27.1 0.8 %combine.1 = bf16[2,64,512]{2,1,0:T(8,128)(2,1)} custom-call(s32[1,2]{1,0:T(1,128)S(1)} %copy-done.1, bf16[128,512]{1,0:T(8,128)(2,1)S(1)} %get-tuple-element.14.refs_0_, bf16[144,512]{1,0:T(8,128)(2,1)S(1)} %collective-permute-done.3.refs_1_, bf16[128,512]{1,0:T(8,128)(2,1)S(1)} %collective-permute-done.4.refs_2_, ...), custom_call_target="tpu_custom_call" | custom-call | tf_op jit(solution)/shard_map/combine/pallas_call | solution.py:232
  27.9 0.1 collective-permute-done.10
  28.0 2.9 %collective-permute-done.9 = f32[1,512]{1,0:T(1,128)S(1)} collective-permute-done((f32[1,512]{1,0:T(1,128)S(1)}, f32[1,512]{1,0:T(1,128)S(1)}, u32[]{:S(2)}, u32[]{:S(2)}) %collective-permute-start.9) | collective-permute-done | bytes 2080 | tf_op jit(solution)/shard_map/ppermute | solution.py:22
  31.0 0.0 collective-permute-done.8
  31.0 0.6 %maximum_maximum_fusion = f32[1,512]{1,0:T(1,128)} fusion(f32[1,512]{1,0:T(1,128)S(1)} %collective-permute-done.10, f32[1,512]{1,0:T(1,128)S(1)} %collective-permute-done.9, f32[1,512]{1,0:T(1,128)S(1)} %max.24, f32[1,512]{1,0:T(1,128)S(1)} %collective-permute-done.8), kind=kLoop, calls=%fused_computation.4 | loop fusion | flops 1536 | bytes 10240 | tf_op jit(solution)/shard_map/max | solution.py:246
  (2 shorter events, 0.0 us)
Async XLA Ops:
  0.6 8.1 %copy-start.1 = (s32[1,2]{1,0:T(1,128)S(1)}, s32[1,2]{1,0:T(1,128)}, u32[]{:S(2)}) copy-start(s32[1,2]{1,0:T(1,128)} %owner_ref.9) | copy-start | bytes 28
  0.6 8.0 %copy-start.3 = (s32[24]{0:T(128)S(1)}, s32[24]{0:T(128)}, u32[]{:S(2)}) copy-start(s32[24]{0:T(128)} %param.9) | copy-start | bytes 292
  0.7 7.3 %collective-permute-start.2 = (bf16[24,512]{1,0:T(8,128)(2,1)}, bf16[24,512]{1,0:T(8,128)(2,1)S(1)}, u32[]{:S(2)}, u32[]{:S(2)}) collective-permute-start(bf16[24,512]{1,0:T(8,128)(2,1)} %refs_1_.1), channel_id=1, source_target_pairs={{0,16},{8,24},{16,0},{24,8},{1,17},{9,25},{17,1},{25,9},{2,18},{10... | collective-permute-start | bytes 73736 | tf_op jit(solution)/shard_map/ppermute | solution.py:22
  3.7 5.0 %collective-permute-start.1 = (bf16[24,512]{1,0:T(8,128)(2,1)}, bf16[24,512]{1,0:T(8,128)(2,1)S(1)}, u32[]{:S(2)}, u32[]{:S(2)}) collective-permute-start(bf16[24,512]{1,0:T(8,128)(2,1)} %refs_1_.1), channel_id=1, source_target_pairs={{0,24},{8,16},{16,8},{24,0},{1,25},{9,17},{17,9},{25,1},{2,26},{10... | collective-permute-start | bytes 73736 | tf_op jit(solution)/shard_map/ppermute | solution.py:22
  5.1 6.0 %collective-permute-start = (bf16[24,512]{1,0:T(8,128)(2,1)}, bf16[24,512]{1,0:T(8,128)(2,1)S(1)}, u32[]{:S(2)}, u32[]{:S(2)}) collective-permute-start(bf16[24,512]{1,0:T(8,128)(2,1)} %refs_1_.1), channel_id=1, source_target_pairs={{0,8},{8,0},{16,24},{24,16},{1,9},{9,1},{17,25},{25,17},{2,10},{10... | collective-permute-start | bytes 73736 | tf_op jit(solution)/shard_map/ppermute | solution.py:22
  5.2 0.7 %copy-start = (s32[1,2]{1,0:T(1,128)S(1)}, s32[1,2]{1,0:T(1,128)}, u32[]{:S(2)}) copy-start(s32[1,2]{1,0:T(1,128)} %slot_ref.1) | copy-start | bytes 28
  5.9 2.8 %copy-start.2 = (bf16[24,512]{1,0:T(8,128)(2,1)S(1)}, bf16[24,512]{1,0:T(8,128)(2,1)}, u32[]{:S(2)}) copy-start(bf16[24,512]{1,0:T(8,128)(2,1)} %refs_1_.1) | copy-start | bytes 73732
  11.0 9.7 %collective-permute-start.5 = (bf16[144,512]{1,0:T(8,128)(2,1)S(1)}, bf16[144,512]{1,0:T(8,128)(2,1)S(1)}, u32[]{:S(2)}, u32[]{:S(2)}) collective-permute-start(bf16[144,512]{1,0:T(8,128)(2,1)S(1)} %correlate.4), channel_id=1, source_target_pairs={{0,24},{8,16},{16,8},{24,0},{1,25},{9,17},{17,9},{25,1},{2,26},{10... | collective-permute-start | bytes 442376 | tf_op jit(solution)/shard_map/ppermute | solution.py:22
  13.4 7.3 %collective-permute-start.3 = (bf16[144,512]{1,0:T(8,128)(2,1)S(1)}, bf16[144,512]{1,0:T(8,128)(2,1)S(1)}, u32[]{:S(2)}, u32[]{:S(2)}) collective-permute-start(bf16[144,512]{1,0:T(8,128)(2,1)S(1)} %correlate.7), channel_id=1, source_target_pairs={{0,8},{8,0},{16,24},{24,16},{1,9},{9,1},{17,25},{25,17},{2,10},{10... | collective-permute-start | bytes 442376 | tf_op jit(solution)/shard_map/ppermute | solution.py:22
  17.0 3.7 %collective-permute-start.6 = (f32[1,512]{1,0:T(1,128)S(1)}, f32[1,512]{1,0:T(1,128)S(1)}, u32[]{:S(2)}, u32[]{:S(2)}) collective-permute-start(f32[1,512]{1,0:T(1,128)S(1)} %get-tuple-element.19), channel_id=1, source_target_pairs={{0,16},{8,24},{16,0},{24,8},{1,17},{9,25},{17,1},{25,9},{2,18},{10... | collective-permute-start | bytes 6152 | tf_op jit(solution)/shard_map/ppermute | solution.py:22
  19.4 7.7 %collective-permute-start.4 = (bf16[128,512]{1,0:T(8,128)(2,1)S(1)}, bf16[128,512]{1,0:T(8,128)(2,1)S(1)}, u32[]{:S(2)}, u32[]{:S(2)}) collective-permute-start(bf16[128,512]{1,0:T(8,128)(2,1)S(1)} %get-tuple-element.17), channel_id=1, source_target_pairs={{0,16},{8,24},{16,0},{24,8},{1,17},{9,25},{17,1},{25,9},{2,18},{10... | collective-permute-start | bytes 393224 | tf_op jit(solution)/shard_map/ppermute | solution.py:22
  20.7 1.2 %collective-permute-start.7 = (f32[1,512]{1,0:T(1,128)S(1)}, f32[1,512]{1,0:T(1,128)S(1)}, u32[]{:S(2)}, u32[]{:S(2)}) collective-permute-start(f32[1,512]{1,0:T(1,128)S(1)} %fusion), channel_id=1, source_target_pairs={{0,1},{1,0},{2,3},{3,2},{4,5},{5,4},{6,7},{7,6},{8,9},{9,8},{10,11... | collective-permute-start | bytes 6152 | tf_op jit(solution)/shard_map/ppermute | solution.py:22
  21.9 6.1 %collective-permute-start.10 = (f32[1,512]{1,0:T(1,128)S(1)}, f32[1,512]{1,0:T(1,128)S(1)}, u32[]{:S(2)}, u32[]{:S(2)}) collective-permute-start(f32[1,512]{1,0:T(1,128)S(1)} %max.24), channel_id=1, source_target_pairs={{0,6},{1,7},{2,4},{3,5},{4,2},{5,3},{6,0},{7,1},{8,14},{9,15},{10,... | collective-permute-start | bytes 6152 | tf_op jit(solution)/shard_map/ppermute | solution.py:22
  26.5 4.5 %collective-permute-start.9 = (f32[1,512]{1,0:T(1,128)S(1)}, f32[1,512]{1,0:T(1,128)S(1)}, u32[]{:S(2)}, u32[]{:S(2)}) collective-permute-start(f32[1,512]{1,0:T(1,128)S(1)} %max.24), channel_id=1, source_target_pairs={{0,4},{1,5},{2,6},{3,7},{4,0},{5,1},{6,2},{7,3},{8,12},{9,13},{10,... | collective-permute-start | bytes 6152 | tf_op jit(solution)/shard_map/ppermute | solution.py:22
  26.5 4.5 %collective-permute-start.8 = (f32[1,512]{1,0:T(1,128)S(1)}, f32[1,512]{1,0:T(1,128)S(1)}, u32[]{:S(2)}, u32[]{:S(2)}) collective-permute-start(f32[1,512]{1,0:T(1,128)S(1)} %max.24), channel_id=1, source_target_pairs={{0,2},{1,3},{2,0},{3,1},{4,6},{5,7},{6,4},{7,5},{8,10},{9,11},{10,... | collective-permute-start | bytes 6152 | tf_op jit(solution)/shard_map/ppermute | solution.py:22
